TPU v7x, 256 devices: a whole 4x4x8 slice. The times are simulated.
256 devices in a mesh: role: 4 (over x), grp: 2 (over y_hi), dev: 32 (over y_lo, z, core).
Axes of the slice: x: 4, y: 4 (y_hi: 2, y_lo: 2; y = y_hi * 2 + y_lo), z: 8, core: 2. Of those that a mesh axis runs over, the one named last changes fastest.
Arguments:
- q_latent: bfloat16 [1536, 2, 128, 512], P(('role', 'grp', 'dev')), may hold values from -256 to 256
- q_rope: bfloat16 [1536, 2, 8192], P(('role', 'grp', 'dev')), may hold values from -256 to 256
- pool_latent: bfloat16 [2, 256, 128, 512], P(None, ('role', 'grp', 'dev')), may hold values from -6 to 6
- pool_rope: bfloat16 [2, 256, 64, 128], P(None, ('role', 'grp', 'dev')), may hold values from -6 to 6
- panel_latent: bfloat16 [1536, 2, 128, 512], P(('role', 'grp', 'dev')), may hold values from -6 to 6
- panel_rope: bfloat16 [1536, 2, 64, 128], P(('role', 'grp', 'dev')), may hold values from -6 to 6
- panel_from: int32 [1536], P(('role', 'grp', 'dev')), may hold values from 0 to 3, as said below
- prefix_id: int32 [1536], P(('role', 'grp', 'dev')), may hold values from 0 to 3
- block_mask: int32 [1536, 16], P(('role', 'grp', 'dev')), may hold values 0 or 1
- suffix_len: int32 [256, 6], P(('role', 'grp', 'dev')), may hold values from 1 to 128, 448 in all within a row
Outputs:
- attended: bfloat16 [1536, 2, 128, 512], P(('role', 'grp', 'dev'))
Inputs may be any that keep to these rules, and one draw needn't show every extreme that they name: For every c < 384, the values panel_from[c + p * 384] over the pools p are a permutation of the pool indices. Among the 6 requests of one device, no pool is named more than 2 times, and some pool is named exactly 2 times.
All inputs are finite; a program needn't handle non-finite values. No bound on the sum of `block_mask` on one device may be relied on, other than what follows from the above.
Results may differ from a plain program's by a relative error of at most 0.0065.
Values may be sent and summed in bfloat16 or wider, within the bound.
No kernel may reach another device: no remote copies, remote signals or barrier semaphores. Data moves between devices by JAX's collectives and lax.ppermute only.
A program may use at most 128 MiB of HBM per device.

v0:
```python
import functools
import math

import jax
import jax.numpy as jnp
from jax import lax
from jax.experimental import pallas as pl
from jax.experimental.pallas import tpu as pltpu
from jax.sharding import Mesh
from jax.sharding import PartitionSpec as P

HEADS = 128
D_LAT = 512
D_ROPE = 64
LAYERS = 2
TILE = 128
ROWS = 144
R_DEV = 6
ROLES = 4
NY = 4
NZ = 8
NAMES = ("role", "yh", "yl", "z", "core")
PLANE = ("yh", "yl", "z", "core")

LOG2E = math.log2(math.e)
LOG2_SCALE = 192.0 ** (-0.5) * LOG2E
NEG = -1e30
OWN_INTS = R_DEV * 19
WIDE = D_LAT + 128

VMEM = pl.BlockSpec(memory_space=pltpu.VMEM)
SMEM = pl.BlockSpec(memory_space=pltpu.SMEM)
ANY = pl.BlockSpec(memory_space=pl.ANY)
BF = jnp.bfloat16
F32 = jnp.float32
SMALL = pltpu.CompilerParams(vmem_limit_bytes=10 << 20)


def unit(*lead):
    return jax.ShapeDtypeStruct(lead + (LAYERS, ROWS, D_LAT), BF)


def pack_into(out, lat, rope):
    out[:TILE, :] = lat[...]
    for j in range(4):
        out[TILE:, 128 * j : 128 * (j + 1)] = rope[16 * j : 16 * (j + 1), :]


def pack_kernel(lat, rope, prefix, length, source, mask, out, ints):
    for layer in range(LAYERS):
        pack_into(out.at[layer], lat.at[layer, 0], rope.at[layer, 0])
    for r in range(R_DEV):
        ints[r] = prefix[r]
        ints[R_DEV + r] = length[0, r]
        ints[2 * R_DEV + r] = source[r]
        for j in range(16):
            ints[3 * R_DEV + 16 * r + j] = mask[r, j]


def pack_blocks(lat, rope, prefix, length, source, mask):
    return pl.pallas_call(
        pack_kernel,
        out_shape=(unit(), jax.ShapeDtypeStruct((OWN_INTS,), jnp.int32)),
        in_specs=[VMEM, VMEM] + [SMEM] * 4,
        out_specs=(VMEM, SMEM),
        name="pack_blocks",
    )(lat, rope, prefix, length, source, mask)


def stack_kernel(n, *refs):
    out = refs[-1]
    for i, ref in enumerate(refs[:n]):
        out[i] = ref[...]


def stack(parts, name, after=()):
    return pl.pallas_call(
        functools.partial(stack_kernel, len(parts)),
        out_shape=unit(len(parts)),
        in_specs=[VMEM] * len(parts) + [ANY] * len(after),
        out_specs=VMEM,
        compiler_params=SMALL,
        name=name,
    )(*parts, *after)


def build_kernel(up_plan, dn_plan, first_up, first_dn, n_parts, up_in, dn_in, *refs):
    parts, (up, dn) = refs[:n_parts], refs[-2:]
    n = up.shape[0]
    core = lax.axis_index("core")

    @pl.when(core == 0)
    def _():
        for i in range(n):
            up[i] = up_in[first_up + i]
            dn[i] = dn_in[first_dn + i]

    @pl.when(core == 1)
    def _():
        for out, plan in ((up, up_plan), (dn, dn_plan)):
            for i in range(n):
                if i < len(plan):
                    kind, index = plan[i]
                    out[i] = {"up": up_in, "dn": dn_in}[kind][index] if kind in ("up", "dn") else parts[index][...]
                else:
                    out[i] = jnp.zeros(out.shape[1:], out.dtype)


def build(up_in, dn_in, parts, up_plan, dn_plan, name, n=4, first_up=0, first_dn=0, after=()):
    return pl.pallas_call(
        functools.partial(build_kernel, up_plan, dn_plan, first_up, first_dn, len(parts)),
        out_shape=(unit(n), unit(n)),
        in_specs=[VMEM] * (2 + len(parts)) + [ANY] * len(after),
        out_specs=(VMEM, VMEM),
        compiler_params=SMALL,
        name=name,
    )(up_in, dn_in, *parts, *after)


def pick_kernel(wanted1, wanted2, wanted3, lat, rope, *outs):
    role = lax.axis_index("role")
    for wanted, out in zip((wanted1, wanted2, wanted3), outs):
        first, second, seen = jnp.int32(0), jnp.int32(0), jnp.int32(0)
        for s in range(R_DEV):
            hit = wanted[s] == role
            first = jnp.where(hit & (seen == 0), s, first)
            second = jnp.where(hit & (seen == 1), s, second)
            seen = seen + hit.astype(jnp.int32)
        for j, slot in enumerate((first, second)):
            for layer in range(LAYERS):
                pack_into(out.at[j, layer], lat.at[slot, layer], rope.at[slot, layer])


def pick_panels(wanted, lat, rope):
    return pl.pallas_call(
        pick_kernel,
        out_shape=(unit(2),) * 3,
        in_specs=[SMEM] * 3 + [VMEM, VMEM],
        out_specs=(VMEM,) * 3,
        compiler_params=SMALL,
        name="pick_panels",
    )(*wanted, lat, rope)


def flash_kernel(plans, panel, halves, first, last, per_step, n_arrays, n_after, *refs):
    refs = list(refs)

    def take(count):
        taken = refs[:count]
        del refs[:count]
        return taken

    ints = take(2)
    queries = [take(2) for _ in halves]
    arrays = take(n_arrays)
    if panel:
        got1, got2, got3, own_lat, own_rope = take(5)
    state_in = None if first else take(2)
    take(n_after)
    state_out = take(2) if not last else None
    out = take(1)[0] if last else None
    scratch = refs
    core, role, row, col = (lax.axis_index(name) for name in ("core", "role", ("yh", "yl"), "z"))

    def prefix(half, r):
        return ints[half][r]

    def length(half, r):
        return ints[half][R_DEV + r]

    def source(r):
        return ints[0][2 * R_DEV + r]

    def live(half, r, block):
        return ints[half][3 * R_DEV + 16 * r + block] == 1

    def one_step(step, carry, which, plan):
        jobs = [(q, h, half) for q in range(per_step) for h, half in enumerate(halves)]

        def keys_of(q, h, layer):
            k = 2 * ((q * len(halves) + h) * LAYERS + layer)
            return scratch[k], scratch[k + 1]

        def put(q, h, i, place, dynamic=None):
            array, index = place
            if dynamic is not None:
                index = dynamic
            for layer in range(LAYERS):
                keys, rope_keys = keys_of(q, h, layer)
                tile = arrays[array].at[layer] if index is None else arrays[array].at[index, layer]
                fill(keys, rope_keys, i, tile)

        def fill(keys, rope_keys, i, tile):
            keys[TILE * i : TILE * (i + 1), :] = tile[:TILE, :]
            for j in range(4):
                rope_keys[16 * j : 16 * (j + 1), TILE * i : TILE * (i + 1)] = tile[TILE:, 128 * j : 128 * (j + 1)]

        def row_of(q, half):
            return (prefix(half, step * per_step + q) - row + NY) % NY

        for q, h, half in jobs:
            dy = row_of(q, half)
            if which == 0:
                slot = jnp.where(dy == 2, 3, jnp.where(dy == 3, 2, dy))
                for i, (_, places) in enumerate(plan):
                    if isinstance(places, int):
                        put(q, h, i, (places, None), slot)
                    else:

                        @pl.when(slot < 2)
                        def _():
                            put(q, h, i, (places[0], None), slot)

                        @pl.when(slot >= 2)
                        def _():
                            put(q, h, i, (places[1], None), slot - 2)

            else:
                for d in range(NY):

                    @pl.when(dy == d)
                    def _():
                        for i, (_, places) in enumerate(plan):
                            put(q, h, i, places[d])

        if panel:
            for q, h, half in jobs:
                if half == 1:
                    continue
                i = len(plan)
                r = step * per_step + q
                shift = (role - source(r) + ROLES) % ROLES
                rank = jnp.int32(0)
                for s in range(R_DEV):
                    rank = rank + ((s < r) & (source(s) == source(r))).astype(jnp.int32)
                rank = jnp.minimum(rank, 1)

                @pl.when(shift == 0)
                def _():
                    for layer in range(LAYERS):
                        keys, rope_keys = keys_of(q, h, layer)
                        keys[TILE * i : TILE * (i + 1), :] = own_lat[r, layer]
                        rope_keys[:, TILE * i : TILE * (i + 1)] = own_rope[r, layer]

                for k, got in enumerate((got1, got2, got3)):

                    @pl.when(shift == k + 1)
                    def _():
                        for layer in range(LAYERS):
                            fill(*keys_of(q, h, layer), i, got.at[rank, layer])

        def chain(q, h, half, layer):
            r = step * per_step + q
            u = 2 * half + layer
            keys, rope_keys = keys_of(q, h, layer)
            n = len(plan) + (1 if panel and half == 0 else 0)
            q_lat, q_rope = queries[h][0][r, layer], queries[h][1][r, layer]
            width = n * TILE
            scores = lax.dot_general(q_lat, keys[:width, :], (((1,), (1,)), ((), ())), preferred_element_type=F32)
            scores = scores + jnp.dot(q_rope, rope_keys[:, :width], preferred_element_type=F32)
            yield
            pieces = []
            for i in range(n):
                piece = scores[:, TILE * i : TILE * (i + 1)] * LOG2_SCALE
                if i == len(plan):
                    token = lax.broadcasted_iota(jnp.int32, (HEADS, TILE), 1)
                    piece = jnp.where(token < length(half, r), piece, NEG)
                else:
                    block = 2 * ((col + (plan[i][0] + NZ)) % NZ) + which
                    piece = piece + jnp.where(live(half, r, block), 0.0, NEG)
                pieces.append(piece)
            top = functools.reduce(jnp.maximum, pieces)
            top = jnp.broadcast_to(jnp.max(top, axis=1, keepdims=True), (HEADS, 128))
            if not first:
                acc_in, ml_in = state_in
                old = ml_in[r, u, :, :128]
                top = jnp.maximum(old, top)
                fade = jnp.exp2(old - top)
            pieces = [jnp.exp2(piece - top) for piece in pieces]
            total = functools.reduce(jnp.add, pieces)
            if not first:
                total = total + fade * ml_in[r, u, :, 128:]
            weights = jnp.concatenate([piece.astype(BF) for piece in pieces], axis=1) if n > 1 else pieces[0].astype(BF)
            yield
            acc = jnp.dot(weights, keys[:width, :], preferred_element_type=F32)
            acc = [acc[:, 128 * j : 128 * (j + 1)] for j in range(4)]
            if not first:
                acc = [acc[j] + acc_in[r, u, :, 128 * j : 128 * (j + 1)] * fade for j in range(4)]
            yield
            if not last:
                acc_out, ml_out = state_out
                for j in range(4):
                    acc_out[r, u, :, 128 * j : 128 * (j + 1)] = acc[j]
                ml_out[r, u, :, :128] = top
                ml_out[r, u, :, 128:] = total
                return
            total = jnp.broadcast_to(jnp.sum(total, axis=1, keepdims=True), (HEADS, 128))
            lse = top + jnp.log(total) * LOG2E
            high = lse.astype(BF).astype(F32)
            mid = (lse - high).astype(BF).astype(F32)
            low = lse - high - mid
            lane = lax.broadcasted_iota(jnp.int32, (HEADS, 128), 1)
            tail = jnp.where(lane == 0, high, jnp.where(lane == 1, mid, jnp.where(lane == 2, low, 0.0)))
            inverse = 1.0 / total
            for j in range(4):
                out[r, layer, :, 128 * j : 128 * (j + 1)] = (acc[j] * inverse).astype(BF)
            out[r, layer, :, D_LAT:] = tail.astype(BF)

        chains = [chain(q, h, half, layer) for q, h, half in jobs for layer in range(LAYERS)]
        for _ in range(3):
            for c in chains:
                next(c)
        for c in chains:
            next(c, None)
        return carry

    for which, plan in enumerate(plans):

        @pl.when(core == which)
        def _():
            lax.fori_loop(0, R_DEV // per_step, functools.partial(one_step, which=which, plan=plan), 0)


def merge_kernel(acc, ml, recv, out):
    for q in range(out.shape[0]):
        r = out.shape[0] * pl.program_id(0) + q
        for layer in range(LAYERS):
            top = ml[r, layer, :, :128]
            total = jnp.broadcast_to(jnp.sum(ml[r, layer, :, 128:], axis=1, keepdims=True), (HEADS, 128))
            tail = recv[r, layer, :, D_LAT:].astype(F32)
            theirs = jnp.broadcast_to(jnp.sum(tail, axis=1, keepdims=True), (HEADS, 128))
            most = jnp.maximum(top, theirs)
            ours, theirs = jnp.exp2(top - most), jnp.exp2(theirs - most)
            scale = 1.0 / (total * ours + theirs)
            ours, theirs = ours * scale, theirs * scale
            for j in range(4):
                cols = slice(128 * j, 128 * (j + 1))
                out[q, layer, :, cols] = (acc[r, layer, :, cols] * ours + recv[r, layer, :, cols].astype(F32) * theirs).astype(BF)


def merge(state, recv):
    return pl.pallas_call(
        merge_kernel,
        grid=(3,),
        out_shape=jax.ShapeDtypeStruct((R_DEV, LAYERS, HEADS, D_LAT), BF),
        in_specs=[VMEM] * 3,
        out_specs=pl.BlockSpec((2, LAYERS, HEADS, D_LAT), lambda i: (i, 0, 0, 0)),
        compiler_params=pltpu.CompilerParams(vmem_limit_bytes=20 << 20),
        name="merge",
    )(*state, recv)


def flash(name, plans, arrays, ints, queries, state=None, panels=None, halves=(0, 1), last=False, after=(), per_step=2):
    first = state is None
    ops = list(ints)
    for half in halves:
        ops += queries[half]
    ops += arrays
    specs = [SMEM] * 2 + [VMEM] * (len(ops) - 2)
    if panels is not None:
        ops += panels
        specs += [VMEM] * 5
    aliases = {}
    if not first:
        if not last:
            aliases = {len(ops): 0, len(ops) + 1: 1}
        ops += state
        specs += [VMEM, VMEM]
    ops += after
    specs += [ANY] * len(after)
    if last:
        out_shape = jax.ShapeDtypeStruct((R_DEV, LAYERS, HEADS, WIDE), BF)
        out_specs = VMEM
    else:
        out_shape = (
            pltpu.VMEM((R_DEV, 2 * LAYERS, HEADS, D_LAT), F32),
            pltpu.VMEM((R_DEV, 2 * LAYERS, HEADS, 256), F32),
        )
        out_specs = (VMEM, VMEM)
    n = max(len(plan) for plan in plans) + (1 if panels is not None else 0)
    tiles = R_DEV * LAYERS * len(halves) * n
    return pl.pallas_call(
        functools.partial(flash_kernel, plans, panels is not None, halves, first, last, per_step, len(arrays), len(after)),
        out_shape=out_shape,
        in_specs=specs,
        out_specs=out_specs,
        scratch_shapes=[pltpu.VMEM((TILE * n, D_LAT), BF), pltpu.VMEM((D_ROPE, TILE * n), BF)]
        * (LAYERS * len(halves) * per_step),
        input_output_aliases=aliases,
        cost_estimate=pl.CostEstimate(
            flops=3 * tiles * HEADS * TILE * (2 * D_LAT + D_ROPE), bytes_accessed=4 << 20, transcendentals=tiles * HEADS * TILE
        ),
        compiler_params=pltpu.CompilerParams(vmem_limit_bytes=20 << 20),
        name=name,
    )(*ops)


def place(y, z, c):
    return ((y % NY) * NZ + z % NZ) * 2 + c


def send(x, moves):
    pairs = [
        (place(y + move[0], z + move[1], c), place(y, z, c))
        for c, move in moves.items()
        for y in range(NY)
        for z in range(NZ)
    ]
    return lax.ppermute(x, PLANE, pairs)


def from_role(x, shift):
    return lax.ppermute(x, "role", [(i, (i - shift) % ROLES) for i in range(ROLES)])


def from_core(x):
    return lax.ppermute(x, "core", [(0, 1), (1, 0)])


def shards(q_latent, q_rope, pool_latent, pool_rope, panel_latent, panel_rope, panel_from, prefix_id, block_mask, suffix_len):
    rope_own = q_rope.reshape(R_DEV, LAYERS, HEADS, D_ROPE)
    own, own_ints = pack_blocks(pool_latent, pool_rope, prefix_id, suffix_len, panel_from, block_mask)

    u0 = send(own, {0: (1, 0), 1: (0, 1)})
    d0 = send(own, {0: (-1, 0), 1: (0, -1)})
    t0 = send(own, {0: (2, 0)})
    a2, a2n = send(u0, {1: (0, 1)}), send(d0, {1: (0, -1)})
    q_own = [q_latent, rope_own]
    m1 = stack([own, u0, d0, t0], "stack1", [rope_own, a2, a2n])

    up, dn = {0: (0, 1), 1: (1, 0)}, {0: (0, -1), 1: (-1, 0)}
    u1, d1 = send(m1, up), send(m1, dn)
    late_latent, late_from, _ = lax.optimization_barrier((q_latent, panel_from, m1))
    wanted = [from_role(late_from, k) for k in (1, 2, 3)]
    lat_par = from_core(late_latent)
    sent = pick_panels(wanted, panel_latent, panel_rope)
    got = [from_role(x, -k) for k, x in zip((1, 2, 3), sent)]

    m2u, m2d = build(
        u1, d1, [a2, a2n], [("x", 0), ("x", 1), ("up", 0), ("up", 1)], [("x", 0), ("x", 1), ("dn", 2)], "build2", after=[*sent, lat_par]
    )
    u2, d2 = send(m2u, up), send(m2d, dn)
    a3, a3n = send(a2, {1: (0, 1)}), send(a2n, {1: (0, -1)})
    late_rope, late_ints, _ = lax.optimization_barrier((rope_own, own_ints, a3))
    q_par = [lat_par, from_core(late_rope)]
    ints = [own_ints, from_core(late_ints)]

    m3u, m3d = build(
        u2,
        d2,
        [a3, a3n],
        [("x", 0), ("x", 1), ("up", 0)],
        [("x", 0), ("x", 1), ("dn", 1)],
        "build3",
        after=[got[1], q_par[1], ints[1]],
    )
    u3, d3 = send(m3u, up), send(m3d, dn)
    a4 = send(a3, {1: (0, 1)})
    queries = (q_own, q_par)
    plans = (
        [(0, 0), (1, 1), (-1, 2), (2, 3), (-2, 4)],
        [
            (0, [(0, 0), (1, 0), (3, 2), (2, 0)]),
            (1, [(0, 1), (1, 1), (3, 3), (2, 1)]),
            (-1, [(0, 2), (1, 2), (4, 2), (2, 2)]),
        ],
    )
    state = flash("flash_near", plans, [m1, u1, d1, u2, d2], ints, queries)

    m4u, m4d = build(
        u3, d3, [a4], [("x", 0), ("up", 0)], [("x", 0), ("dn", 1)], "build4", 2, 0, 2, [got[0], got[2], state[1]]
    )
    u4, d4 = send(m4u, up), send(m4d, dn)
    t4 = send(a4, {1: (2, 0)})
    plans = (
        [(3, 2), (-3, 3)],
        [(2, [(4, None), (0, 0), (2, 2), (1, 0)]), (-2, [(5, None), (0, 1), (3, 2), (1, 1)])],
    )
    state = flash(
        "flash_mid", plans, [u2, d2, u3, d3, a2, a2n], ints, queries, state, [*got, panel_latent, panel_rope]
    )

    plans = (
        [(4, (2, 3))],
        [
            (3, [(4, None), (0, 0), (2, 1), (1, 0)]),
            (-3, [(5, None), (0, 1), (3, 1), (1, 1)]),
            (4, [(6, None), (2, 0), (7, None), (3, 0)]),
        ],
    )
    arrays = [u3, d3, u4, d4, a3, a3n, a4, t4]
    part = flash("flash_far_par", plans, arrays, ints, queries, state, None, (1,), True, per_step=3)
    state = flash("flash_far_own", plans, arrays, ints, queries, state, None, (0,), False, [part], per_step=3)
    return merge(state, from_core(part))


def solution(mesh):
    fine = Mesh(mesh.devices.reshape(ROLES, 2, 2, NZ, 2), NAMES)
    rows = P(NAMES)
    blocks = P(None, NAMES)
    return jax.shard_map(
        shards,
        mesh=fine,
        in_specs=(rows, rows, blocks, blocks, rows, rows, rows, rows, rows, rows),
        out_specs=rows,
        check_vma=False,
    )
```

profile of v0, /device:TPU:1, one launch (start us, length us, event | category | flops | bytes accessed | tf_op | source)
XLA Modules:
  0.0 110.6 jit_solution(8838509950635442716)
XLA Ops:
  0.0 1.7 %pack_blocks.1 = (bf16[2,144,512]{2,1,0:T(8,128)(2,1)}, s32[114]{0:T(128)}) custom-call(bf16[2,1,128,512]{3,2,1,0:T(8,128)(2,1)} %lat.2, bf16[2,1,64,128]{3,2,1,0:T(8,128)(2,1)} %rope.2, s32[6]{0:T(128)} %prefix.1, s32[1,6]{1,0:T(1,128)} %length.1, s32[6]{0:T(128)} %source.1, s32[6,16]{1,0:T(8,128)} %mask.1), custom_call_target="tpu_custom_call" | custom-call | tf_op jit(solution)/shard_map/pack_blocks/pallas_call | solution.py:61
  1.7 6.5 %collective-permute-start = (bf16[2,144,512]{2,1,0:T(8,128)(2,1)}, bf16[2,144,512]{2,1,0:T(8,128)(2,1)S(1)}, u32[]{:S(2)}, u32[]{:S(2)}) collective-permute-start(bf16[2,144,512]{2,1,0:T(8,128)(2,1)} %get-tuple-element.27.refs_0_), channel_id=1, source_target_pairs={{16,0},{18,2},{20,4},{22,6},{24,8},{26,10},{28,12},{30,14},{32,16}... | collective-permute-start | bytes 884744 | tf_op jit(solution)/shard_map/ppermute | solution.py:409
  8.9 3.3 %collective-permute-done.refs_1_ = bf16[2,144,512]{2,1,0:T(8,128)(2,1)S(1)} collective-permute-done((bf16[2,144,512]{2,1,0:T(8,128)(2,1)}, bf16[2,144,512]{2,1,0:T(8,128)(2,1)S(1)}, u32[]{:S(2)}, u32[]{:S(2)}) %collective-permute-start) | collective-permute-done | bytes 294944 | tf_op jit(solution)/shard_map/ppermute | solution.py:409
  12.2 4.9 %collective-permute-start.1 = (bf16[2,144,512]{2,1,0:T(8,128)(2,1)S(1)}, bf16[2,144,512]{2,1,0:T(8,128)(2,1)S(1)}, u32[]{:S(2)}, u32[]{:S(2)}) collective-permute-start(bf16[2,144,512]{2,1,0:T(8,128)(2,1)S(1)} %collective-permute-done.refs_1_), channel_id=1, source_target_pairs={{3,1},{5,3},{7,5},{9,7},{11,9},{13,11},{15,13},{1,15},{19,17},{21,... | collective-permute-start | bytes 884744 | tf_op jit(solution)/shard_map/ppermute | solution.py:409
  17.1 1.9 %collective-permute-start.6 = (bf16[2,144,512]{2,1,0:T(8,128)(2,1)S(1)}, bf16[2,144,512]{2,1,0:T(8,128)(2,1)S(1)}, u32[]{:S(2)}, u32[]{:S(2)}) collective-permute-start(bf16[2,144,512]{2,1,0:T(8,128)(2,1)S(1)} %collective-permute-done.4.refs_2_), channel_id=1, source_target_pairs={{15,1},{1,3},{3,5},{5,7},{7,9},{9,11},{11,13},{13,15},{31,17},{17,... | collective-permute-start | bytes 884744 | tf_op jit(solution)/shard_map/ppermute | solution.py:409
  19.1 1.2 %reshape.3.refs_4_.refs_3_ = bf16[6,2,128,64]{3,2,1,0:T(8,128)(2,1)S(1)} reshape(bf16[6,2,8192]{2,1,0:T(2,128)(2,1)} %param.11) | data formatting | bytes 393216 | tf_op jit(solution)/shard_map/reshape | solution.py:421
  20.7 5.0 %collective-permute-done.6.refs_6_.refs_1_.refs_11_ = bf16[2,144,512]{2,1,0:T(8,128)(2,1)S(1)} collective-permute-done((bf16[2,144,512]{2,1,0:T(8,128)(2,1)S(1)}, bf16[2,144,512]{2,1,0:T(8,128)(2,1)S(1)}, u32[]{:S(2)}, u32[]{:S(2)}) %collective-permute-start.6) | collective-permute-done | bytes 294944 | tf_op jit(solution)/shard_map/ppermute | solution.py:409
  26.9 3.1 %collective-permute-start.7 = (bf16[4,2,144,512]{3,2,1,0:T(8,128)(2,1)S(1)}, bf16[4,2,144,512]{3,2,1,0:T(8,128)(2,1)S(1)}, u32[]{:S(2)}, u32[]{:S(2)}) collective-permute-start(bf16[4,2,144,512]{3,2,1,0:T(8,128)(2,1)S(1)} %stack1.1.refs_6_), channel_id=1, source_target_pairs={{2,0},{4,2},{6,4},{8,6},{10,8},{12,10},{14,12},{0,14},{18,16},{20,... | collective-permute-start | bytes 3538952 | tf_op jit(solution)/shard_map/ppermute | solution.py:409
  30.1 2.7 %collective-permute-start.10 = (s32[6]{0:T(128)S(1)}, s32[6]{0:T(128)S(1)}, u32[]{:S(2)}, u32[]{:S(2)}) collective-permute-start(s32[6]{0:T(128)S(1)} %copy-done.5), channel_id=1, source_target_pairs={{0,128},{64,192},{128,0},{192,64},{1,129},{65,193},{129,1},{193,65... | collective-permute-start | bytes 80 | tf_op jit(solution)/shard_map/ppermute | solution.py:413
  34.0 2.5 %collective-permute-start.9 = (s32[6]{0:T(128)S(1)}, s32[6]{0:T(128)S(1)}, u32[]{:S(2)}, u32[]{:S(2)}) collective-permute-start(s32[6]{0:T(128)S(1)} %copy-done.5), channel_id=1, source_target_pairs={{0,192},{64,0},{128,64},{192,128},{1,193},{65,1},{129,65},{193,129... | collective-permute-start | bytes 80 | tf_op jit(solution)/shard_map/ppermute | solution.py:413
  37.9 5.3 %collective-permute-done.7.up_in.refs_7_ = bf16[4,2,144,512]{3,2,1,0:T(8,128)(2,1)S(1)} collective-permute-done((bf16[4,2,144,512]{3,2,1,0:T(8,128)(2,1)S(1)}, bf16[4,2,144,512]{3,2,1,0:T(8,128)(2,1)S(1)}, u32[]{:S(2)}, u32[]{:S(2)}) %collective-permute-start.7) | collective-permute-done | bytes 1179680 | tf_op jit(solution)/shard_map/ppermute | solution.py:409
  43.2 3.1 %collective-permute-done.8.dn_in.refs_8_ = bf16[4,2,144,512]{3,2,1,0:T(8,128)(2,1)S(1)} collective-permute-done((bf16[4,2,144,512]{3,2,1,0:T(8,128)(2,1)S(1)}, bf16[4,2,144,512]{3,2,1,0:T(8,128)(2,1)S(1)}, u32[]{:S(2)}, u32[]{:S(2)}) %collective-permute-start.8) | collective-permute-done | bytes 1179680 | tf_op jit(solution)/shard_map/ppermute | solution.py:409
  48.0 2.7 %collective-permute-start.16 = (bf16[2,2,144,512]{3,2,1,0:T(8,128)(2,1)S(1)}, bf16[2,2,144,512]{3,2,1,0:T(8,128)(2,1)S(1)}, u32[]{:S(2)}, u32[]{:S(2)}) collective-permute-start(bf16[2,2,144,512]{3,2,1,0:T(8,128)(2,1)S(1)} %get-tuple-element.31.refs_3_), channel_id=1, source_target_pairs={{0,128},{64,192},{128,0},{192,64},{1,129},{65,193},{129,1},{193,65... | collective-permute-start | bytes 1769480 | tf_op jit(solution)/shard_map/ppermute | solution.py:413
  50.8 1.9 %collective-permute-start.2 = (bf16[2,144,512]{2,1,0:T(8,128)(2,1)S(1)}, bf16[2,144,512]{2,1,0:T(8,128)(2,1)S(1)}, u32[]{:S(2)}, u32[]{:S(2)}) collective-permute-start(bf16[2,144,512]{2,1,0:T(8,128)(2,1)S(1)} %collective-permute-done.1.refs_5_.refs_0_.refs_10_), channel_id=1, source_target_pairs={{3,1},{5,3},{7,5},{9,7},{11,9},{13,11},{15,13},{1,15},{19,17},{21,... | collective-permute-start | bytes 884744 | tf_op jit(solution)/shard_map/ppermute | solution.py:409
  52.7 3.4 %collective-permute-start.15 = (bf16[2,144,512]{2,1,0:T(8,128)(2,1)S(1)}, bf16[2,144,512]{2,1,0:T(8,128)(2,1)S(1)}, u32[]{:S(2)}, u32[]{:S(2)}) collective-permute-start(bf16[2,144,512]{2,1,0:T(8,128)(2,1)S(1)} %collective-permute-done.6.refs_6_.refs_1_.refs_11_), channel_id=1, source_target_pairs={{15,1},{1,3},{3,5},{5,7},{7,9},{9,11},{11,13},{13,15},{31,17},{17,... | collective-permute-start | bytes 884744 | tf_op jit(solution)/shard_map/ppermute | solution.py:409
  56.1 5.7 %collective-permute-done.2.refs_0_.refs_8_ = bf16[2,144,512]{2,1,0:T(8,128)(2,1)S(1)} collective-permute-done((bf16[2,144,512]{2,1,0:T(8,128)(2,1)S(1)}, bf16[2,144,512]{2,1,0:T(8,128)(2,1)S(1)}, u32[]{:S(2)}, u32[]{:S(2)}) %collective-permute-start.2) | collective-permute-done | bytes 294944 | tf_op jit(solution)/shard_map/ppermute | solution.py:409
  61.7 3.1 %collective-permute-done.15.refs_1_.refs_9_ = bf16[2,144,512]{2,1,0:T(8,128)(2,1)S(1)} collective-permute-done((bf16[2,144,512]{2,1,0:T(8,128)(2,1)S(1)}, bf16[2,144,512]{2,1,0:T(8,128)(2,1)S(1)}, u32[]{:S(2)}, u32[]{:S(2)}) %collective-permute-start.15) | collective-permute-done | bytes 294944 | tf_op jit(solution)/shard_map/ppermute | solution.py:409
  66.2 1.6 %collective-permute-start.18 = (bf16[4,2,144,512]{3,2,1,0:T(8,128)(2,1)S(1)}, bf16[4,2,144,512]{3,2,1,0:T(8,128)(2,1)S(1)}, u32[]{:S(2)}, u32[]{:S(2)}) collective-permute-start(bf16[4,2,144,512]{3,2,1,0:T(8,128)(2,1)S(1)} %get-tuple-element.37), channel_id=1, source_target_pairs={{2,0},{4,2},{6,4},{8,6},{10,8},{12,10},{14,12},{0,14},{18,16},{20,... | collective-permute-start | bytes 3538952 | tf_op jit(solution)/shard_map/ppermute | solution.py:409
  68.1 2.4 %collective-permute-start.22 = (bf16[2,2,144,512]{3,2,1,0:T(8,128)(2,1)S(1)}, bf16[2,2,144,512]{3,2,1,0:T(8,128)(2,1)S(1)}, u32[]{:S(2)}, u32[]{:S(2)}) collective-permute-start(bf16[2,2,144,512]{3,2,1,0:T(8,128)(2,1)S(1)} %get-tuple-element.32.refs_4_), channel_id=1, source_target_pairs={{0,192},{64,0},{128,64},{192,128},{1,193},{65,1},{129,65},{193,129... | collective-permute-start | bytes 1769480 | tf_op jit(solution)/shard_map/ppermute | solution.py:413
  70.5 1.9 %collective-permute-start.20 = (bf16[2,144,512]{2,1,0:T(8,128)(2,1)S(1)}, bf16[2,144,512]{2,1,0:T(8,128)(2,1)S(1)}, u32[]{:S(2)}, u32[]{:S(2)}) collective-permute-start(bf16[2,144,512]{2,1,0:T(8,128)(2,1)S(1)} %collective-permute-done.2.refs_0_.refs_8_), channel_id=1, source_target_pairs={{3,1},{5,3},{7,5},{9,7},{11,9},{13,11},{15,13},{1,15},{19,17},{21,... | collective-permute-start | bytes 884744 | tf_op jit(solution)/shard_map/ppermute | solution.py:409
  72.4 7.2 %flash_near.1 = (f32[6,4,128,512]{3,2,1,0:T(8,128)S(1)}, f32[6,4,128,256]{3,2,1,0:T(8,128)S(1)}) custom-call(s32[114]{0:T(128)S(1)} %copy-done.4, s32[114]{0:T(128)S(1)} %collective-permute-done.3.refs_4_.refs_1_, bf16[6,2,128,512]{3,2,1,0:T(8,128)(2,1)S(1)} %copy-done, bf16[6,2,128,64]{3,2,1,0:T(8,128)(2,1)S(1)} %reshape.3.refs_4_.refs_3_, ...), custom_call_target="tpu_custom_call" | custom-call | flops 6417285120 | bytes 4194304 | tf_op jit(solution)/shard_map/flash_near/pallas_call | solution.py:382
  79.6 1.9 %collective-permute-done.20.refs_0_.refs_10_ = bf16[2,144,512]{2,1,0:T(8,128)(2,1)S(1)} collective-permute-done((bf16[2,144,512]{2,1,0:T(8,128)(2,1)S(1)}, bf16[2,144,512]{2,1,0:T(8,128)(2,1)S(1)}, u32[]{:S(2)}, u32[]{:S(2)}) %collective-permute-start.20) | collective-permute-done | bytes 294944 | tf_op jit(solution)/shard_map/ppermute | solution.py:409
  81.5 1.7 %collective-permute-done.21.refs_1_.refs_12_ = bf16[2,2,144,512]{3,2,1,0:T(8,128)(2,1)S(1)} collective-permute-done((bf16[2,2,144,512]{3,2,1,0:T(8,128)(2,1)S(1)}, bf16[2,2,144,512]{3,2,1,0:T(8,128)(2,1)S(1)}, u32[]{:S(2)}, u32[]{:S(2)}) %collective-permute-start.21) | collective-permute-done | bytes 589856 | tf_op jit(solution)/shard_map/ppermute | solution.py:413
  83.2 1.2 %collective-permute-done.19.dn_in.refs_9_.refs_5_ = bf16[4,2,144,512]{3,2,1,0:T(8,128)(2,1)S(1)} collective-permute-done((bf16[4,2,144,512]{3,2,1,0:T(8,128)(2,1)S(1)}, bf16[4,2,144,512]{3,2,1,0:T(8,128)(2,1)S(1)}, u32[]{:S(2)}, u32[]{:S(2)}) %collective-permute-start.19) | collective-permute-done | bytes 1179680 | tf_op jit(solution)/shard_map/ppermute | solution.py:409
  84.5 1.7 %collective-permute-start.23 = (bf16[2,2,144,512]{3,2,1,0:T(8,128)(2,1)S(1)}, bf16[2,2,144,512]{3,2,1,0:T(8,128)(2,1)S(1)}, u32[]{:S(2)}, u32[]{:S(2)}) collective-permute-start(bf16[2,2,144,512]{3,2,1,0:T(8,128)(2,1)S(1)} %get-tuple-element.40), channel_id=1, source_target_pairs={{2,0},{4,2},{6,4},{8,6},{10,8},{12,10},{14,12},{0,14},{18,16},{20,... | collective-permute-start | bytes 1769480 | tf_op jit(solution)/shard_map/ppermute | solution.py:409
  86.2 3.2 %collective-permute-start.25 = (bf16[2,144,512]{2,1,0:T(8,128)(2,1)S(1)}, bf16[2,144,512]{2,1,0:T(8,128)(2,1)S(1)}, u32[]{:S(2)}, u32[]{:S(2)}) collective-permute-start(bf16[2,144,512]{2,1,0:T(8,128)(2,1)S(1)} %collective-permute-done.20.refs_0_.refs_10_), channel_id=1, source_target_pairs={{33,1},{35,3},{37,5},{39,7},{41,9},{43,11},{45,13},{47,15},{49,17}... | collective-permute-start | bytes 884744 | tf_op jit(solution)/shard_map/ppermute | solution.py:409
  89.4 7.0 %flash_mid.1 = (f32[6,4,128,512]{3,2,1,0:T(8,128)S(1)}, f32[6,4,128,256]{3,2,1,0:T(8,128)S(1)}) custom-call(s32[114]{0:T(128)S(1)} %copy-done.4, s32[114]{0:T(128)S(1)} %collective-permute-done.3.refs_4_.refs_1_, bf16[6,2,128,512]{3,2,1,0:T(8,128)(2,1)S(1)} %copy-done, ...), custom_call_target="tpu_custom_call", output_to_operand_aliasing={{0}: (17, {}), {1}: (18, {})} | custom-call | flops 3850371072 | bytes 4194304 | tf_op jit(solution)/shard_map/flash_mid/pallas_call | solution.py:382
  96.4 1.6 %collective-permute-done.25.refs_11_ = bf16[2,144,512]{2,1,0:T(8,128)(2,1)S(1)} collective-permute-done((bf16[2,144,512]{2,1,0:T(8,128)(2,1)S(1)}, bf16[2,144,512]{2,1,0:T(8,128)(2,1)S(1)}, u32[]{:S(2)}, u32[]{:S(2)}) %collective-permute-start.25) | collective-permute-done | bytes 294944 | tf_op jit(solution)/shard_map/ppermute | solution.py:409
  98.0 1.3 %collective-permute-done.24.refs_7_ = bf16[2,2,144,512]{3,2,1,0:T(8,128)(2,1)S(1)} collective-permute-done((bf16[2,2,144,512]{3,2,1,0:T(8,128)(2,1)S(1)}, bf16[2,2,144,512]{3,2,1,0:T(8,128)(2,1)S(1)}, u32[]{:S(2)}, u32[]{:S(2)}) %collective-permute-start.24) | collective-permute-done | bytes 589856 | tf_op jit(solution)/shard_map/ppermute | solution.py:409
  99.3 4.5 %flash_far_par.1.refs_14_ = bf16[6,2,128,640]{3,2,1,0:T(8,128)(2,1)S(1)} custom-call(s32[114]{0:T(128)S(1)} %copy-done.4, s32[114]{0:T(128)S(1)} %collective-permute-done.3.refs_4_.refs_1_, bf16[6,2,128,512]{3,2,1,0:T(8,128)(2,1)S(1)} %collective-permute-done.12.refs_5_.refs_4_.refs_2_, bf16[6,2,128,64]{3,2,1,0:T(8,128)(2,1)S(1)} %collective-permute-done.17.refs_3_.refs_5_, ...), custom_call_target="tpu_custom_call" | custom-call | flops 1925185536 | bytes 4194304 | tf_op jit(solution)/shard_map/flash_far_par/pallas_call | solution.py:382
  103.9 4.2 %flash_far_own.1 = (f32[6,4,128,512]{3,2,1,0:T(8,128)S(1)}, f32[6,4,128,256]{3,2,1,0:T(8,128)S(1)}) custom-call(s32[114]{0:T(128)S(1)} %copy-done.4, s32[114]{0:T(128)S(1)} %collective-permute-done.3.refs_4_.refs_1_, bf16[6,2,128,512]{3,2,1,0:T(8,128)(2,1)S(1)} %copy-done, ...), custom_call_target="tpu_custom_call", output_to_operand_aliasing={{0}: (12, {}), {1}: (13, {})} | custom-call | flops 1925185536 | bytes 4194304 | tf_op jit(solution)/shard_map/flash_far_own/pallas_call | solution.py:382
  108.2 2.4 %merge.1 = bf16[6,2,128,512]{3,2,1,0:T(8,128)(2,1)} custom-call(f32[6,4,128,512]{3,2,1,0:T(8,128)S(1)} %get-tuple-element.45.acc, f32[6,4,128,256]{3,2,1,0:T(8,128)S(1)} %get-tuple-element.46.ml, bf16[6,2,128,640]{3,2,1,0:T(8,128)(2,1)S(1)} %collective-permute-done.26.recv), custom_call_target="tpu_custom_call" | custom-call | tf_op jit(solution)/shard_map/merge/pallas_call | solution.py:342
  (46 shorter events, 8.4 us)
Async XLA Ops:
  1.7 10.5 %collective-permute-start = (bf16[2,144,512]{2,1,0:T(8,128)(2,1)}, bf16[2,144,512]{2,1,0:T(8,128)(2,1)S(1)}, u32[]{:S(2)}, u32[]{:S(2)}) collective-permute-start(bf16[2,144,512]{2,1,0:T(8,128)(2,1)} %get-tuple-element.27.refs_0_), channel_id=1, source_target_pairs={{16,0},{18,2},{20,4},{22,6},{24,8},{26,10},{28,12},{30,14},{32,16}... | collective-permute-start | bytes 884744 | tf_op jit(solution)/shard_map/ppermute | solution.py:409
  8.2 8.9 %collective-permute-start.4 = (bf16[2,144,512]{2,1,0:T(8,128)(2,1)}, bf16[2,144,512]{2,1,0:T(8,128)(2,1)S(1)}, u32[]{:S(2)}, u32[]{:S(2)}) collective-permute-start(bf16[2,144,512]{2,1,0:T(8,128)(2,1)} %get-tuple-element.27.refs_0_), channel_id=1, source_target_pairs={{48,0},{50,2},{52,4},{54,6},{56,8},{58,10},{60,12},{62,14},{0,16},... | collective-permute-start | bytes 884744 | tf_op jit(solution)/shard_map/ppermute | solution.py:409
  8.2 12.1 %collective-permute-start.5 = (bf16[2,144,512]{2,1,0:T(8,128)(2,1)}, bf16[2,144,512]{2,1,0:T(8,128)(2,1)S(1)}, u32[]{:S(2)}, u32[]{:S(2)}) collective-permute-start(bf16[2,144,512]{2,1,0:T(8,128)(2,1)} %get-tuple-element.27.refs_0_), channel_id=1, source_target_pairs={{32,0},{34,2},{36,4},{38,6},{40,8},{42,10},{44,12},{46,14},{48,16}... | collective-permute-start | bytes 884744 | tf_op jit(solution)/shard_map/ppermute | solution.py:409
  12.2 8.6 %collective-permute-start.1 = (bf16[2,144,512]{2,1,0:T(8,128)(2,1)S(1)}, bf16[2,144,512]{2,1,0:T(8,128)(2,1)S(1)}, u32[]{:S(2)}, u32[]{:S(2)}) collective-permute-start(bf16[2,144,512]{2,1,0:T(8,128)(2,1)S(1)} %collective-permute-done.refs_1_), channel_id=1, source_target_pairs={{3,1},{5,3},{7,5},{9,7},{11,9},{13,11},{15,13},{1,15},{19,17},{21,... | collective-permute-start | bytes 884744 | tf_op jit(solution)/shard_map/ppermute | solution.py:409
  17.1 8.7 %collective-permute-start.6 = (bf16[2,144,512]{2,1,0:T(8,128)(2,1)S(1)}, bf16[2,144,512]{2,1,0:T(8,128)(2,1)S(1)}, u32[]{:S(2)}, u32[]{:S(2)}) collective-permute-start(bf16[2,144,512]{2,1,0:T(8,128)(2,1)S(1)} %collective-permute-done.4.refs_2_), channel_id=1, source_target_pairs={{15,1},{1,3},{3,5},{5,7},{7,9},{9,11},{11,13},{13,15},{31,17},{17,... | collective-permute-start | bytes 884744 | tf_op jit(solution)/shard_map/ppermute | solution.py:409
  19.0 11.0 %copy-start.5 = (s32[6]{0:T(128)S(1)}, s32[6]{0:T(128)}, u32[]{:S(2)}) copy-start(s32[6]{0:T(128)} %source.1) | copy-start | bytes 76
  20.3 6.6 %copy-start = (bf16[6,2,128,512]{3,2,1,0:T(8,128)(2,1)S(1)}, bf16[6,2,128,512]{3,2,1,0:T(8,128)(2,1)}, u32[]{:S(2)}) copy-start(bf16[6,2,128,512]{3,2,1,0:T(8,128)(2,1)} %refs_2_.5) | copy-start | bytes 4718596
  20.3 16.9 %copy-start.1 = (bf16[6,2,128,512]{3,2,1,0:T(8,128)(2,1)S(1)}, bf16[6,2,128,512]{3,2,1,0:T(8,128)(2,1)}, u32[]{:S(2)}) copy-start(bf16[6,2,128,512]{3,2,1,0:T(8,128)(2,1)} %refs_15_.1) | copy-start | bytes 4718596
  20.3 16.9 %copy-start.2 = (bf16[6,2,64,128]{3,2,1,0:T(8,128)(2,1)S(1)}, bf16[6,2,64,128]{3,2,1,0:T(8,128)(2,1)}, u32[]{:S(2)}) copy-start(bf16[6,2,64,128]{3,2,1,0:T(8,128)(2,1)} %refs_16_.1) | copy-start | bytes 589828
  26.8 19.5 %collective-permute-start.12 = (bf16[6,2,128,512]{3,2,1,0:T(8,128)(2,1)S(1)}, bf16[6,2,128,512]{3,2,1,0:T(8,128)(2,1)S(1)}, u32[]{:S(2)}, u32[]{:S(2)}) collective-permute-start(bf16[6,2,128,512]{3,2,1,0:T(8,128)(2,1)S(1)} %copy-done), channel_id=1, source_target_pairs={{0,1},{1,0},{2,3},{3,2},{4,5},{5,4},{6,7},{7,6},{8,9},{9,8},{10,11... | collective-permute-start | bytes 4718600 | tf_op jit(solution)/shard_map/ppermute | solution.py:417
  26.9 16.3 %collective-permute-start.7 = (bf16[4,2,144,512]{3,2,1,0:T(8,128)(2,1)S(1)}, bf16[4,2,144,512]{3,2,1,0:T(8,128)(2,1)S(1)}, u32[]{:S(2)}, u32[]{:S(2)}) collective-permute-start(bf16[4,2,144,512]{3,2,1,0:T(8,128)(2,1)S(1)} %stack1.1.refs_6_), channel_id=1, source_target_pairs={{2,0},{4,2},{6,4},{8,6},{10,8},{12,10},{14,12},{0,14},{18,16},{20,... | collective-permute-start | bytes 3538952 | tf_op jit(solution)/shard_map/ppermute | solution.py:409
  30.1 16.3 %collective-permute-start.8 = (bf16[4,2,144,512]{3,2,1,0:T(8,128)(2,1)S(1)}, bf16[4,2,144,512]{3,2,1,0:T(8,128)(2,1)S(1)}, u32[]{:S(2)}, u32[]{:S(2)}) collective-permute-start(bf16[4,2,144,512]{3,2,1,0:T(8,128)(2,1)S(1)} %stack1.1.refs_6_), channel_id=1, source_target_pairs={{14,0},{0,2},{2,4},{4,6},{6,8},{8,10},{10,12},{12,14},{30,16},{16,... | collective-permute-start | bytes 3538952 | tf_op jit(solution)/shard_map/ppermute | solution.py:409
  30.1 3.9 %collective-permute-start.10 = (s32[6]{0:T(128)S(1)}, s32[6]{0:T(128)S(1)}, u32[]{:S(2)}, u32[]{:S(2)}) collective-permute-start(s32[6]{0:T(128)S(1)} %copy-done.5), channel_id=1, source_target_pairs={{0,128},{64,192},{128,0},{192,64},{1,129},{65,193},{129,1},{193,65... | collective-permute-start | bytes 80 | tf_op jit(solution)/shard_map/ppermute | solution.py:413
  32.8 3.9 %collective-permute-start.11 = (s32[6]{0:T(128)S(1)}, s32[6]{0:T(128)S(1)}, u32[]{:S(2)}, u32[]{:S(2)}) collective-permute-start(s32[6]{0:T(128)S(1)} %copy-done.5), channel_id=1, source_target_pairs={{0,64},{64,128},{128,192},{192,0},{1,65},{65,129},{129,193},{193,1... | collective-permute-start | bytes 80 | tf_op jit(solution)/shard_map/ppermute | solution.py:413
  34.0 3.2 %collective-permute-start.9 = (s32[6]{0:T(128)S(1)}, s32[6]{0:T(128)S(1)}, u32[]{:S(2)}, u32[]{:S(2)}) collective-permute-start(s32[6]{0:T(128)S(1)} %copy-done.5), channel_id=1, source_target_pairs={{0,192},{64,0},{128,64},{192,128},{1,193},{65,1},{129,65},{193,129... | collective-permute-start | bytes 80 | tf_op jit(solution)/shard_map/ppermute | solution.py:413
  46.3 18.6 %copy-start.4 = (s32[114]{0:T(128)S(1)}, s32[114]{0:T(128)}, u32[]{:S(2)}) copy-start(s32[114]{0:T(128)} %get-tuple-element.28.refs_0_) | copy-start | bytes 1372
  46.5 19.5 %collective-permute-start.13 = (bf16[4,2,144,512]{3,2,1,0:T(8,128)(2,1)S(1)}, bf16[4,2,144,512]{3,2,1,0:T(8,128)(2,1)S(1)}, u32[]{:S(2)}, u32[]{:S(2)}) collective-permute-start(bf16[4,2,144,512]{3,2,1,0:T(8,128)(2,1)S(1)} %get-tuple-element.34), channel_id=1, source_target_pairs={{2,0},{4,2},{6,4},{8,6},{10,8},{12,10},{14,12},{0,14},{18,16},{20,... | collective-permute-start | bytes 3538952 | tf_op jit(solution)/shard_map/ppermute | solution.py:409
  46.9 19.1 %collective-permute-start.14 = (bf16[4,2,144,512]{3,2,1,0:T(8,128)(2,1)S(1)}, bf16[4,2,144,512]{3,2,1,0:T(8,128)(2,1)S(1)}, u32[]{:S(2)}, u32[]{:S(2)}) collective-permute-start(bf16[4,2,144,512]{3,2,1,0:T(8,128)(2,1)S(1)} %get-tuple-element.35), channel_id=1, source_target_pairs={{14,0},{0,2},{2,4},{4,6},{6,8},{8,10},{10,12},{12,14},{30,16},{16,... | collective-permute-start | bytes 3538952 | tf_op jit(solution)/shard_map/ppermute | solution.py:409
  48.0 18.0 %collective-permute-start.16 = (bf16[2,2,144,512]{3,2,1,0:T(8,128)(2,1)S(1)}, bf16[2,2,144,512]{3,2,1,0:T(8,128)(2,1)S(1)}, u32[]{:S(2)}, u32[]{:S(2)}) collective-permute-start(bf16[2,2,144,512]{3,2,1,0:T(8,128)(2,1)S(1)} %get-tuple-element.31.refs_3_), channel_id=1, source_target_pairs={{0,128},{64,192},{128,0},{192,64},{1,129},{65,193},{129,1},{193,65... | collective-permute-start | bytes 1769480 | tf_op jit(solution)/shard_map/ppermute | solution.py:413
  50.8 11.0 %collective-permute-start.2 = (bf16[2,144,512]{2,1,0:T(8,128)(2,1)S(1)}, bf16[2,144,512]{2,1,0:T(8,128)(2,1)S(1)}, u32[]{:S(2)}, u32[]{:S(2)}) collective-permute-start(bf16[2,144,512]{2,1,0:T(8,128)(2,1)S(1)} %collective-permute-done.1.refs_5_.refs_0_.refs_10_), channel_id=1, source_target_pairs={{3,1},{5,3},{7,5},{9,7},{11,9},{13,11},{15,13},{1,15},{19,17},{21,... | collective-permute-start | bytes 884744 | tf_op jit(solution)/shard_map/ppermute | solution.py:409
  52.7 12.2 %collective-permute-start.15 = (bf16[2,144,512]{2,1,0:T(8,128)(2,1)S(1)}, bf16[2,144,512]{2,1,0:T(8,128)(2,1)S(1)}, u32[]{:S(2)}, u32[]{:S(2)}) collective-permute-start(bf16[2,144,512]{2,1,0:T(8,128)(2,1)S(1)} %collective-permute-done.6.refs_6_.refs_1_.refs_11_), channel_id=1, source_target_pairs={{15,1},{1,3},{3,5},{5,7},{7,9},{9,11},{11,13},{13,15},{31,17},{17,... | collective-permute-start | bytes 884744 | tf_op jit(solution)/shard_map/ppermute | solution.py:409
  61.7 4.3 %collective-permute-start.17 = (bf16[6,2,128,64]{3,2,1,0:T(8,128)(2,1)S(1)}, bf16[6,2,128,64]{3,2,1,0:T(8,128)(2,1)S(1)}, u32[]{:S(2)}, u32[]{:S(2)}) collective-permute-start(bf16[6,2,128,64]{3,2,1,0:T(8,128)(2,1)S(1)} %reshape.3.refs_4_.refs_3_), channel_id=1, source_target_pairs={{0,1},{1,0},{2,3},{3,2},{4,5},{5,4},{6,7},{7,6},{8,9},{9,8},{10,11... | collective-permute-start | bytes 589832 | tf_op jit(solution)/shard_map/ppermute | solution.py:417
  64.9 1.1 %collective-permute-start.3 = (s32[114]{0:T(128)S(1)}, s32[114]{0:T(128)S(1)}, u32[]{:S(2)}, u32[]{:S(2)}) collective-permute-start(s32[114]{0:T(128)S(1)} %copy-done.4), channel_id=1, source_target_pairs={{0,1},{1,0},{2,3},{3,2},{4,5},{5,4},{6,7},{7,6},{8,9},{9,8},{10,11... | collective-permute-start | bytes 1376 | tf_op jit(solution)/shard_map/ppermute | solution.py:417
  66.2 17.0 %collective-permute-start.18 = (bf16[4,2,144,512]{3,2,1,0:T(8,128)(2,1)S(1)}, bf16[4,2,144,512]{3,2,1,0:T(8,128)(2,1)S(1)}, u32[]{:S(2)}, u32[]{:S(2)}) collective-permute-start(bf16[4,2,144,512]{3,2,1,0:T(8,128)(2,1)S(1)} %get-tuple-element.37), channel_id=1, source_target_pairs={{2,0},{4,2},{6,4},{8,6},{10,8},{12,10},{14,12},{0,14},{18,16},{20,... | collective-permute-start | bytes 3538952 | tf_op jit(solution)/shard_map/ppermute | solution.py:409
  67.8 16.6 %collective-permute-start.19 = (bf16[4,2,144,512]{3,2,1,0:T(8,128)(2,1)S(1)}, bf16[4,2,144,512]{3,2,1,0:T(8,128)(2,1)S(1)}, u32[]{:S(2)}, u32[]{:S(2)}) collective-permute-start(bf16[4,2,144,512]{3,2,1,0:T(8,128)(2,1)S(1)} %get-tuple-element.38), channel_id=1, source_target_pairs={{14,0},{0,2},{2,4},{4,6},{6,8},{8,10},{10,12},{12,14},{30,16},{16,... | collective-permute-start | bytes 3538952 | tf_op jit(solution)/shard_map/ppermute | solution.py:409
  67.8 15.4 %collective-permute-start.21 = (bf16[2,2,144,512]{3,2,1,0:T(8,128)(2,1)S(1)}, bf16[2,2,144,512]{3,2,1,0:T(8,128)(2,1)S(1)}, u32[]{:S(2)}, u32[]{:S(2)}) collective-permute-start(bf16[2,2,144,512]{3,2,1,0:T(8,128)(2,1)S(1)} %get-tuple-element.30.refs_2_), channel_id=1, source_target_pairs={{0,64},{64,128},{128,192},{192,0},{1,65},{65,129},{129,193},{193,1... | collective-permute-start | bytes 1769480 | tf_op jit(solution)/shard_map/ppermute | solution.py:413
  68.1 15.1 %collective-permute-start.22 = (bf16[2,2,144,512]{3,2,1,0:T(8,128)(2,1)S(1)}, bf16[2,2,144,512]{3,2,1,0:T(8,128)(2,1)S(1)}, u32[]{:S(2)}, u32[]{:S(2)}) collective-permute-start(bf16[2,2,144,512]{3,2,1,0:T(8,128)(2,1)S(1)} %get-tuple-element.32.refs_4_), channel_id=1, source_target_pairs={{0,192},{64,0},{128,64},{192,128},{1,193},{65,1},{129,65},{193,129... | collective-permute-start | bytes 1769480 | tf_op jit(solution)/shard_map/ppermute | solution.py:413
  70.5 11.0 %collective-permute-start.20 = (bf16[2,144,512]{2,1,0:T(8,128)(2,1)S(1)}, bf16[2,144,512]{2,1,0:T(8,128)(2,1)S(1)}, u32[]{:S(2)}, u32[]{:S(2)}) collective-permute-start(bf16[2,144,512]{2,1,0:T(8,128)(2,1)S(1)} %collective-permute-done.2.refs_0_.refs_8_), channel_id=1, source_target_pairs={{3,1},{5,3},{7,5},{9,7},{11,9},{13,11},{15,13},{1,15},{19,17},{21,... | collective-permute-start | bytes 884744 | tf_op jit(solution)/shard_map/ppermute | solution.py:409
  84.5 13.6 %collective-permute-start.23 = (bf16[2,2,144,512]{3,2,1,0:T(8,128)(2,1)S(1)}, bf16[2,2,144,512]{3,2,1,0:T(8,128)(2,1)S(1)}, u32[]{:S(2)}, u32[]{:S(2)}) collective-permute-start(bf16[2,2,144,512]{3,2,1,0:T(8,128)(2,1)S(1)} %get-tuple-element.40), channel_id=1, source_target_pairs={{2,0},{4,2},{6,4},{8,6},{10,8},{12,10},{14,12},{0,14},{18,16},{20,... | collective-permute-start | bytes 1769480 | tf_op jit(solution)/shard_map/ppermute | solution.py:409
  86.2 13.1 %collective-permute-start.24 = (bf16[2,2,144,512]{3,2,1,0:T(8,128)(2,1)S(1)}, bf16[2,2,144,512]{3,2,1,0:T(8,128)(2,1)S(1)}, u32[]{:S(2)}, u32[]{:S(2)}) collective-permute-start(bf16[2,2,144,512]{3,2,1,0:T(8,128)(2,1)S(1)} %get-tuple-element.41), channel_id=1, source_target_pairs={{14,0},{0,2},{2,4},{4,6},{6,8},{8,10},{10,12},{12,14},{30,16},{16,... | collective-permute-start | bytes 1769480 | tf_op jit(solution)/shard_map/ppermute | solution.py:409
  86.2 11.8 %collective-permute-start.25 = (bf16[2,144,512]{2,1,0:T(8,128)(2,1)S(1)}, bf16[2,144,512]{2,1,0:T(8,128)(2,1)S(1)}, u32[]{:S(2)}, u32[]{:S(2)}) collective-permute-start(bf16[2,144,512]{2,1,0:T(8,128)(2,1)S(1)} %collective-permute-done.20.refs_0_.refs_10_), channel_id=1, source_target_pairs={{33,1},{35,3},{37,5},{39,7},{41,9},{43,11},{45,13},{47,15},{49,17}... | collective-permute-start | bytes 884744 | tf_op jit(solution)/shard_map/ppermute | solution.py:409
  103.8 4.3 %collective-permute-start.26 = (bf16[6,2,128,640]{3,2,1,0:T(8,128)(2,1)S(1)}, bf16[6,2,128,640]{3,2,1,0:T(8,128)(2,1)S(1)}, u32[]{:S(2)}, u32[]{:S(2)}) collective-permute-start(bf16[6,2,128,640]{3,2,1,0:T(8,128)(2,1)S(1)} %flash_far_par.1.refs_14_), channel_id=1, source_target_pairs={{0,1},{1,0},{2,3},{3,2},{4,5},{5,4},{6,7},{7,6},{8,9},{9,8},{10,11... | collective-permute-start | bytes 5898248 | tf_op jit(solution)/shard_map/ppermute | solution.py:417
  (1 other events, 1.0 us)
where the time goes:
time: 111 us
  starting transfers between devices  43.5 us (39%)
  waiting for transfers between devices  36.4 us (33%)
  Pallas kernels  28.2 us (25%)
  local copies, waits for them, and re-layouts  2.2 us (2%)
    ppermute x17, starting transfers between devices, send(): return lax.ppermute(x, PLANE, pairs)  32.3 us
    ppermute x17, waiting for transfers between devices, send(): return lax.ppermute(x, PLANE, pairs)  32 us
    pallas_call x4, Pallas kernels, flash(): pl.pallas_call(functools.partial(flash_kernel, plans, panels is not None,...  23 us
    ppermute x6, starting transfers between devices, from_role(): lax.ppermute(x, 'role', [(i, (i - shift) % ROLES) for i in range(ROLES)])  11 us
    ppermute x6, waiting for transfers between devices, from_role(): lax.ppermute(x, 'role', [(i, (i - shift) % ROLES) for i in range(ROLES)])  3.28 us
    pallas_call x1, Pallas kernels, merge(): pl.pallas_call(merge_kernel, grid=(3,), out_shape=jax.ShapeDtypeStruct((R...  2.4 us
  transfers between devices with their start and end apart: 27, of which 16 were waited for; matrix products, arithmetic and copies ran while one was open for 1% of the time, Pallas kernels for 17%

commit v1 on v0

--- a/solution.py
+++ b/solution.py
@@ -426,18 +426,18 @@
     t0 = send(own, {0: (2, 0)})
     a2, a2n = send(u0, {1: (0, 1)}), send(d0, {1: (0, -1)})
     q_own = [q_latent, rope_own]
-    m1 = stack([own, u0, d0, t0], "stack1", [rope_own, a2, a2n])
+    lat_par = from_core(q_latent)
+    m1 = stack([own, u0, d0, t0], "stack1", [rope_own, a2, a2n, lat_par])
 
     up, dn = {0: (0, 1), 1: (1, 0)}, {0: (0, -1), 1: (-1, 0)}
     u1, d1 = send(m1, up), send(m1, dn)
-    late_latent, late_from, _ = lax.optimization_barrier((q_latent, panel_from, m1))
+    late_from, _ = lax.optimization_barrier((panel_from, m1))
     wanted = [from_role(late_from, k) for k in (1, 2, 3)]
-    lat_par = from_core(late_latent)
     sent = pick_panels(wanted, panel_latent, panel_rope)
     got = [from_role(x, -k) for k, x in zip((1, 2, 3), sent)]
 
     m2u, m2d = build(
-        u1, d1, [a2, a2n], [("x", 0), ("x", 1), ("up", 0), ("up", 1)], [("x", 0), ("x", 1), ("dn", 2)], "build2", after=[*sent, lat_par]
+        u1, d1, [a2, a2n], [("x", 0), ("x", 1), ("up", 0), ("up", 1)], [("x", 0), ("x", 1), ("dn", 2)], "build2", after=sent
     )
     u2, d2 = send(m2u, up), send(m2d, dn)
     a3, a3n = send(a2, {1: (0, 1)}), send(a2n, {1: (0, -1)})

time: 111 us -> 111 us (level)
  starting transfers between devices: 43.5 us -> 40.7 us
  waiting for transfers between devices: 36.4 us -> 39 us
    ppermute x6, waiting for transfers between devices: 3.28 us -> 9.96 us  [from_role(): lax.ppermute(x, 'role', [(i, (i - shift) % ROLES) for i in range(ROLES)])]
    ppermute x17, starting transfers between devices: 32.3 us -> 28.2 us  [send(): return lax.ppermute(x, PLANE, pairs)]
    ppermute x17, waiting for transfers between devices: 32 us -> 27.9 us  [send(): return lax.ppermute(x, PLANE, pairs)]
    ppermute x4, starting transfers between devices: 0.19 us -> 3.34 us  [from_core(): return lax.ppermute(x, 'core', [(0, 1), (1, 0)])]
    ppermute x6, starting transfers between devices: 11 us -> 9.1 us  [from_role(): lax.ppermute(x, 'role', [(i, (i - shift) % ROLES) for i in range(ROLES)])]
  transfers between devices with their start and end apart: 27 -> 27, of which waited for: 16 -> 13; matrix products, arithmetic and copies ran while one was open for 1% -> 1% of each run, Pallas kernels for 17% -> 19%
where the time goes in v1:
time: 111 us; the launch traced here: 110 us
  starting transfers between devices  40.7 us (37%)
  waiting for transfers between devices  39 us (35%)
  Pallas kernels  28.3 us (25%)
  local copies, waits for them, and re-layouts  2.2 us (2%)
    ppermute x17, starting transfers between devices, send(): return lax.ppermute(x, PLANE, pairs)  28.2 us
    ppermute x17, waiting for transfers between devices, send(): return lax.ppermute(x, PLANE, pairs)  27.9 us
    pallas_call x4, Pallas kernels, flash(): pl.pallas_call(functools.partial(flash_kernel, plans, panels is not None,...  22.9 us
    ppermute x6, waiting for transfers between devices, from_role(): lax.ppermute(x, 'role', [(i, (i - shift) % ROLES) for i in range(ROLES)])  9.96 us
    ppermute x6, starting transfers between devices, from_role(): lax.ppermute(x, 'role', [(i, (i - shift) % ROLES) for i in range(ROLES)])  9.1 us
    ppermute x4, starting transfers between devices, from_core(): return lax.ppermute(x, 'core', [(0, 1), (1, 0)])  3.34 us
    pallas_call x1, Pallas kernels, merge(): pl.pallas_call(merge_kernel, grid=(3,), out_shape=jax.ShapeDtypeStruct((R...  2.41 us
  transfers between devices with their start and end apart: 27, of which 13 were waited for; matrix products, arithmetic and copies ran while one was open for 1% of the time, Pallas kernels for 19%

profile of v1, /device:TPU:1, one launch (start us, length us, event | category | flops | bytes accessed | tf_op | source)
XLA Modules:
  0.0 110.4 jit_solution(7312745785704903013)
XLA Ops:
  0.0 3.2 %collective-permute-start.7 = (bf16[6,2,128,512]{3,2,1,0:T(8,128)(2,1)}, bf16[6,2,128,512]{3,2,1,0:T(8,128)(2,1)S(1)}, u32[]{:S(2)}, u32[]{:S(2)}) collective-permute-start(bf16[6,2,128,512]{3,2,1,0:T(8,128)(2,1)} %refs_2_.5), channel_id=1, source_target_pairs={{0,1},{1,0},{2,3},{3,2},{4,5},{5,4},{6,7},{7,6},{8,9},{9,8},{10,11... | collective-permute-start | bytes 4718600 | tf_op jit(solution)/shard_map/ppermute | solution.py:417
  3.2 1.7 %pack_blocks.1 = (bf16[2,144,512]{2,1,0:T(8,128)(2,1)}, s32[114]{0:T(128)}) custom-call(bf16[2,1,128,512]{3,2,1,0:T(8,128)(2,1)} %lat.2, bf16[2,1,64,128]{3,2,1,0:T(8,128)(2,1)} %rope.2, s32[6]{0:T(128)} %prefix.1, s32[1,6]{1,0:T(1,128)} %length.1, s32[6]{0:T(128)} %source.1, s32[6,16]{1,0:T(8,128)} %mask.1), custom_call_target="tpu_custom_call" | custom-call | tf_op jit(solution)/shard_map/pack_blocks/pallas_call | solution.py:61
  5.0 3.9 %collective-permute-start = (bf16[2,144,512]{2,1,0:T(8,128)(2,1)}, bf16[2,144,512]{2,1,0:T(8,128)(2,1)S(1)}, u32[]{:S(2)}, u32[]{:S(2)}) collective-permute-start(bf16[2,144,512]{2,1,0:T(8,128)(2,1)} %get-tuple-element.26.refs_0_), channel_id=1, source_target_pairs={{16,0},{18,2},{20,4},{22,6},{24,8},{26,10},{28,12},{30,14},{32,16}... | collective-permute-start | bytes 884744 | tf_op jit(solution)/shard_map/ppermute | solution.py:409
  9.6 3.3 %collective-permute-done.refs_1_ = bf16[2,144,512]{2,1,0:T(8,128)(2,1)S(1)} collective-permute-done((bf16[2,144,512]{2,1,0:T(8,128)(2,1)}, bf16[2,144,512]{2,1,0:T(8,128)(2,1)S(1)}, u32[]{:S(2)}, u32[]{:S(2)}) %collective-permute-start) | collective-permute-done | bytes 294944 | tf_op jit(solution)/shard_map/ppermute | solution.py:409
  12.9 4.9 %collective-permute-start.1 = (bf16[2,144,512]{2,1,0:T(8,128)(2,1)S(1)}, bf16[2,144,512]{2,1,0:T(8,128)(2,1)S(1)}, u32[]{:S(2)}, u32[]{:S(2)}) collective-permute-start(bf16[2,144,512]{2,1,0:T(8,128)(2,1)S(1)} %collective-permute-done.refs_1_), channel_id=1, source_target_pairs={{3,1},{5,3},{7,5},{9,7},{11,9},{13,11},{15,13},{1,15},{19,17},{21,... | collective-permute-start | bytes 884744 | tf_op jit(solution)/shard_map/ppermute | solution.py:409
  17.8 1.9 %collective-permute-start.6 = (bf16[2,144,512]{2,1,0:T(8,128)(2,1)S(1)}, bf16[2,144,512]{2,1,0:T(8,128)(2,1)S(1)}, u32[]{:S(2)}, u32[]{:S(2)}) collective-permute-start(bf16[2,144,512]{2,1,0:T(8,128)(2,1)S(1)} %collective-permute-done.4.refs_2_), channel_id=1, source_target_pairs={{15,1},{1,3},{3,5},{5,7},{7,9},{9,11},{11,13},{13,15},{31,17},{17,... | collective-permute-start | bytes 884744 | tf_op jit(solution)/shard_map/ppermute | solution.py:409
  21.4 5.0 %collective-permute-done.6.refs_6_.refs_1_.refs_11_ = bf16[2,144,512]{2,1,0:T(8,128)(2,1)S(1)} collective-permute-done((bf16[2,144,512]{2,1,0:T(8,128)(2,1)S(1)}, bf16[2,144,512]{2,1,0:T(8,128)(2,1)S(1)}, u32[]{:S(2)}, u32[]{:S(2)}) %collective-permute-start.6) | collective-permute-done | bytes 294944 | tf_op jit(solution)/shard_map/ppermute | solution.py:409
  27.5 3.1 %collective-permute-start.8 = (bf16[4,2,144,512]{3,2,1,0:T(8,128)(2,1)S(1)}, bf16[4,2,144,512]{3,2,1,0:T(8,128)(2,1)S(1)}, u32[]{:S(2)}, u32[]{:S(2)}) collective-permute-start(bf16[4,2,144,512]{3,2,1,0:T(8,128)(2,1)S(1)} %stack1.1.refs_6_), channel_id=1, source_target_pairs={{2,0},{4,2},{6,4},{8,6},{10,8},{12,10},{14,12},{0,14},{18,16},{20,... | collective-permute-start | bytes 3538952 | tf_op jit(solution)/shard_map/ppermute | solution.py:409
  30.6 2.5 %collective-permute-start.10 = (s32[6]{0:T(128)S(1)}, s32[6]{0:T(128)S(1)}, u32[]{:S(2)}, u32[]{:S(2)}) collective-permute-start(s32[6]{0:T(128)S(1)} %copy-done.5), channel_id=1, source_target_pairs={{0,192},{64,0},{128,64},{192,128},{1,193},{65,1},{129,65},{193,129... | collective-permute-start | bytes 80 | tf_op jit(solution)/shard_map/ppermute | solution.py:413
  34.2 2.8 %collective-permute-done.11.wanted2 = s32[6]{0:T(128)S(1)} collective-permute-done((s32[6]{0:T(128)S(1)}, s32[6]{0:T(128)S(1)}, u32[]{:S(2)}, u32[]{:S(2)}) %collective-permute-start.11) | collective-permute-done | bytes 56 | tf_op jit(solution)/shard_map/ppermute | solution.py:413
  38.2 5.5 %collective-permute-done.8.up_in.refs_7_ = bf16[4,2,144,512]{3,2,1,0:T(8,128)(2,1)S(1)} collective-permute-done((bf16[4,2,144,512]{3,2,1,0:T(8,128)(2,1)S(1)}, bf16[4,2,144,512]{3,2,1,0:T(8,128)(2,1)S(1)}, u32[]{:S(2)}, u32[]{:S(2)}) %collective-permute-start.8) | collective-permute-done | bytes 1179680 | tf_op jit(solution)/shard_map/ppermute | solution.py:409
  43.8 3.1 %collective-permute-done.9.dn_in.refs_8_ = bf16[4,2,144,512]{3,2,1,0:T(8,128)(2,1)S(1)} collective-permute-done((bf16[4,2,144,512]{3,2,1,0:T(8,128)(2,1)S(1)}, bf16[4,2,144,512]{3,2,1,0:T(8,128)(2,1)S(1)}, u32[]{:S(2)}, u32[]{:S(2)}) %collective-permute-start.9) | collective-permute-done | bytes 1179680 | tf_op jit(solution)/shard_map/ppermute | solution.py:409
  47.1 1.5 %collective-permute-start.14 = (bf16[4,2,144,512]{3,2,1,0:T(8,128)(2,1)S(1)}, bf16[4,2,144,512]{3,2,1,0:T(8,128)(2,1)S(1)}, u32[]{:S(2)}, u32[]{:S(2)}) collective-permute-start(bf16[4,2,144,512]{3,2,1,0:T(8,128)(2,1)S(1)} %get-tuple-element.33), channel_id=1, source_target_pairs={{14,0},{0,2},{2,4},{4,6},{6,8},{8,10},{10,12},{12,14},{30,16},{16,... | collective-permute-start | bytes 3538952 | tf_op jit(solution)/shard_map/ppermute | solution.py:409
  48.6 2.7 %collective-permute-start.16 = (bf16[2,2,144,512]{3,2,1,0:T(8,128)(2,1)S(1)}, bf16[2,2,144,512]{3,2,1,0:T(8,128)(2,1)S(1)}, u32[]{:S(2)}, u32[]{:S(2)}) collective-permute-start(bf16[2,2,144,512]{3,2,1,0:T(8,128)(2,1)S(1)} %get-tuple-element.30.refs_3_), channel_id=1, source_target_pairs={{0,128},{64,192},{128,0},{192,64},{1,129},{65,193},{129,1},{193,65... | collective-permute-start | bytes 1769480 | tf_op jit(solution)/shard_map/ppermute | solution.py:413
  51.3 1.9 %collective-permute-start.2 = (bf16[2,144,512]{2,1,0:T(8,128)(2,1)S(1)}, bf16[2,144,512]{2,1,0:T(8,128)(2,1)S(1)}, u32[]{:S(2)}, u32[]{:S(2)}) collective-permute-start(bf16[2,144,512]{2,1,0:T(8,128)(2,1)S(1)} %collective-permute-done.1.refs_5_.refs_0_.refs_10_), channel_id=1, source_target_pairs={{3,1},{5,3},{7,5},{9,7},{11,9},{13,11},{15,13},{1,15},{19,17},{21,... | collective-permute-start | bytes 884744 | tf_op jit(solution)/shard_map/ppermute | solution.py:409
  53.2 3.4 %collective-permute-start.15 = (bf16[2,144,512]{2,1,0:T(8,128)(2,1)S(1)}, bf16[2,144,512]{2,1,0:T(8,128)(2,1)S(1)}, u32[]{:S(2)}, u32[]{:S(2)}) collective-permute-start(bf16[2,144,512]{2,1,0:T(8,128)(2,1)S(1)} %collective-permute-done.6.refs_6_.refs_1_.refs_11_), channel_id=1, source_target_pairs={{15,1},{1,3},{3,5},{5,7},{7,9},{9,11},{11,13},{13,15},{31,17},{17,... | collective-permute-start | bytes 884744 | tf_op jit(solution)/shard_map/ppermute | solution.py:409
  56.6 5.7 %collective-permute-done.2.refs_0_.refs_8_ = bf16[2,144,512]{2,1,0:T(8,128)(2,1)S(1)} collective-permute-done((bf16[2,144,512]{2,1,0:T(8,128)(2,1)S(1)}, bf16[2,144,512]{2,1,0:T(8,128)(2,1)S(1)}, u32[]{:S(2)}, u32[]{:S(2)}) %collective-permute-start.2) | collective-permute-done | bytes 294944 | tf_op jit(solution)/shard_map/ppermute | solution.py:409
  62.3 2.0 %collective-permute-done.15.refs_1_.refs_9_ = bf16[2,144,512]{2,1,0:T(8,128)(2,1)S(1)} collective-permute-done((bf16[2,144,512]{2,1,0:T(8,128)(2,1)S(1)}, bf16[2,144,512]{2,1,0:T(8,128)(2,1)S(1)}, u32[]{:S(2)}, u32[]{:S(2)}) %collective-permute-start.15) | collective-permute-done | bytes 294944 | tf_op jit(solution)/shard_map/ppermute | solution.py:409
  65.7 1.5 %collective-permute-start.19 = (bf16[4,2,144,512]{3,2,1,0:T(8,128)(2,1)S(1)}, bf16[4,2,144,512]{3,2,1,0:T(8,128)(2,1)S(1)}, u32[]{:S(2)}, u32[]{:S(2)}) collective-permute-start(bf16[4,2,144,512]{3,2,1,0:T(8,128)(2,1)S(1)} %get-tuple-element.36), channel_id=1, source_target_pairs={{14,0},{0,2},{2,4},{4,6},{6,8},{8,10},{10,12},{12,14},{30,16},{16,... | collective-permute-start | bytes 3538952 | tf_op jit(solution)/shard_map/ppermute | solution.py:409
  67.2 1.9 %collective-permute-start.20 = (bf16[2,144,512]{2,1,0:T(8,128)(2,1)S(1)}, bf16[2,144,512]{2,1,0:T(8,128)(2,1)S(1)}, u32[]{:S(2)}, u32[]{:S(2)}) collective-permute-start(bf16[2,144,512]{2,1,0:T(8,128)(2,1)S(1)} %collective-permute-done.2.refs_0_.refs_8_), channel_id=1, source_target_pairs={{3,1},{5,3},{7,5},{9,7},{11,9},{13,11},{15,13},{1,15},{19,17},{21,... | collective-permute-start | bytes 884744 | tf_op jit(solution)/shard_map/ppermute | solution.py:409
  69.1 1.5 %collective-permute-start.21 = (bf16[2,2,144,512]{3,2,1,0:T(8,128)(2,1)S(1)}, bf16[2,2,144,512]{3,2,1,0:T(8,128)(2,1)S(1)}, u32[]{:S(2)}, u32[]{:S(2)}) collective-permute-start(bf16[2,2,144,512]{3,2,1,0:T(8,128)(2,1)S(1)} %get-tuple-element.29.refs_2_), channel_id=1, source_target_pairs={{0,64},{64,128},{128,192},{192,0},{1,65},{65,129},{129,193},{193,1... | collective-permute-start | bytes 1769480 | tf_op jit(solution)/shard_map/ppermute | solution.py:413
  70.6 1.2 %collective-permute-start.22 = (bf16[2,2,144,512]{3,2,1,0:T(8,128)(2,1)S(1)}, bf16[2,2,144,512]{3,2,1,0:T(8,128)(2,1)S(1)}, u32[]{:S(2)}, u32[]{:S(2)}) collective-permute-start(bf16[2,2,144,512]{3,2,1,0:T(8,128)(2,1)S(1)} %get-tuple-element.31.refs_4_), channel_id=1, source_target_pairs={{0,192},{64,0},{128,64},{192,128},{1,193},{65,1},{129,65},{193,129... | collective-permute-start | bytes 1769480 | tf_op jit(solution)/shard_map/ppermute | solution.py:413
  71.9 7.2 %flash_near.1 = (f32[6,4,128,512]{3,2,1,0:T(8,128)S(1)}, f32[6,4,128,256]{3,2,1,0:T(8,128)S(1)}) custom-call(s32[114]{0:T(128)S(1)} %copy-done.4, s32[114]{0:T(128)S(1)} %collective-permute-done.3.refs_4_.refs_1_, bf16[6,2,128,512]{3,2,1,0:T(8,128)(2,1)S(1)} %copy-done, bf16[6,2,128,64]{3,2,1,0:T(8,128)(2,1)S(1)} %reshape.3.refs_4_.refs_3_, ...), custom_call_target="tpu_custom_call" | custom-call | flops 6417285120 | bytes 4194304 | tf_op jit(solution)/shard_map/flash_near/pallas_call | solution.py:382
  79.1 6.7 %collective-permute-done.21.refs_1_.refs_12_ = bf16[2,2,144,512]{3,2,1,0:T(8,128)(2,1)S(1)} collective-permute-done((bf16[2,2,144,512]{3,2,1,0:T(8,128)(2,1)S(1)}, bf16[2,2,144,512]{3,2,1,0:T(8,128)(2,1)S(1)}, u32[]{:S(2)}, u32[]{:S(2)}) %collective-permute-start.21) | collective-permute-done | bytes 589856 | tf_op jit(solution)/shard_map/ppermute | solution.py:413
  85.9 1.5 %collective-permute-start.24 = (bf16[2,2,144,512]{3,2,1,0:T(8,128)(2,1)S(1)}, bf16[2,2,144,512]{3,2,1,0:T(8,128)(2,1)S(1)}, u32[]{:S(2)}, u32[]{:S(2)}) collective-permute-start(bf16[2,2,144,512]{3,2,1,0:T(8,128)(2,1)S(1)} %get-tuple-element.39), channel_id=1, source_target_pairs={{14,0},{0,2},{2,4},{4,6},{6,8},{8,10},{10,12},{12,14},{30,16},{16,... | collective-permute-start | bytes 1769480 | tf_op jit(solution)/shard_map/ppermute | solution.py:409
  87.4 1.9 %collective-permute-start.25 = (bf16[2,144,512]{2,1,0:T(8,128)(2,1)S(1)}, bf16[2,144,512]{2,1,0:T(8,128)(2,1)S(1)}, u32[]{:S(2)}, u32[]{:S(2)}) collective-permute-start(bf16[2,144,512]{2,1,0:T(8,128)(2,1)S(1)} %collective-permute-done.20.refs_0_.refs_10_), channel_id=1, source_target_pairs={{33,1},{35,3},{37,5},{39,7},{41,9},{43,11},{45,13},{47,15},{49,17}... | collective-permute-start | bytes 884744 | tf_op jit(solution)/shard_map/ppermute | solution.py:409
  89.3 7.0 %flash_mid.1 = (f32[6,4,128,512]{3,2,1,0:T(8,128)S(1)}, f32[6,4,128,256]{3,2,1,0:T(8,128)S(1)}) custom-call(s32[114]{0:T(128)S(1)} %copy-done.4, s32[114]{0:T(128)S(1)} %collective-permute-done.3.refs_4_.refs_1_, bf16[6,2,128,512]{3,2,1,0:T(8,128)(2,1)S(1)} %copy-done, ...), custom_call_target="tpu_custom_call", output_to_operand_aliasing={{0}: (17, {}), {1}: (18, {})} | custom-call | flops 3850371072 | bytes 4194304 | tf_op jit(solution)/shard_map/flash_mid/pallas_call | solution.py:382
  96.3 1.3 %collective-permute-done.25.refs_11_ = bf16[2,144,512]{2,1,0:T(8,128)(2,1)S(1)} collective-permute-done((bf16[2,144,512]{2,1,0:T(8,128)(2,1)S(1)}, bf16[2,144,512]{2,1,0:T(8,128)(2,1)S(1)}, u32[]{:S(2)}, u32[]{:S(2)}) %collective-permute-start.25) | collective-permute-done | bytes 294944 | tf_op jit(solution)/shard_map/ppermute | solution.py:409
  97.6 1.5 %collective-permute-done.24.refs_7_ = bf16[2,2,144,512]{3,2,1,0:T(8,128)(2,1)S(1)} collective-permute-done((bf16[2,2,144,512]{3,2,1,0:T(8,128)(2,1)S(1)}, bf16[2,2,144,512]{3,2,1,0:T(8,128)(2,1)S(1)}, u32[]{:S(2)}, u32[]{:S(2)}) %collective-permute-start.24) | collective-permute-done | bytes 589856 | tf_op jit(solution)/shard_map/ppermute | solution.py:409
  99.1 4.5 %flash_far_par.1.refs_14_ = bf16[6,2,128,640]{3,2,1,0:T(8,128)(2,1)S(1)} custom-call(s32[114]{0:T(128)S(1)} %copy-done.4, s32[114]{0:T(128)S(1)} %collective-permute-done.3.refs_4_.refs_1_, bf16[6,2,128,512]{3,2,1,0:T(8,128)(2,1)S(1)} %collective-permute-done.7.refs_7_.refs_4_.refs_2_, bf16[6,2,128,64]{3,2,1,0:T(8,128)(2,1)S(1)} %collective-permute-done.17.refs_3_.refs_5_, ...), custom_call_target="tpu_custom_call" | custom-call | flops 1925185536 | bytes 4194304 | tf_op jit(solution)/shard_map/flash_far_par/pallas_call | solution.py:382
  103.7 4.2 %flash_far_own.1 = (f32[6,4,128,512]{3,2,1,0:T(8,128)S(1)}, f32[6,4,128,256]{3,2,1,0:T(8,128)S(1)}) custom-call(s32[114]{0:T(128)S(1)} %copy-done.4, s32[114]{0:T(128)S(1)} %collective-permute-done.3.refs_4_.refs_1_, bf16[6,2,128,512]{3,2,1,0:T(8,128)(2,1)S(1)} %copy-done, ...), custom_call_target="tpu_custom_call", output_to_operand_aliasing={{0}: (12, {}), {1}: (13, {})} | custom-call | flops 1925185536 | bytes 4194304 | tf_op jit(solution)/shard_map/flash_far_own/pallas_call | solution.py:382
  108.0 2.4 %merge.1 = bf16[6,2,128,512]{3,2,1,0:T(8,128)(2,1)} custom-call(f32[6,4,128,512]{3,2,1,0:T(8,128)S(1)} %get-tuple-element.43.acc, f32[6,4,128,256]{3,2,1,0:T(8,128)S(1)} %get-tuple-element.44.ml, bf16[6,2,128,640]{3,2,1,0:T(8,128)(2,1)S(1)} %collective-permute-done.26.recv), custom_call_target="tpu_custom_call" | custom-call | tf_op jit(solution)/shard_map/merge/pallas_call | solution.py:342
  (46 shorter events, 7.7 us)
Async XLA Ops:
  0.0 26.5 %collective-permute-start.7 = (bf16[6,2,128,512]{3,2,1,0:T(8,128)(2,1)}, bf16[6,2,128,512]{3,2,1,0:T(8,128)(2,1)S(1)}, u32[]{:S(2)}, u32[]{:S(2)}) collective-permute-start(bf16[6,2,128,512]{3,2,1,0:T(8,128)(2,1)} %refs_2_.5), channel_id=1, source_target_pairs={{0,1},{1,0},{2,3},{3,2},{4,5},{5,4},{6,7},{7,6},{8,9},{9,8},{10,11... | collective-permute-start | bytes 4718600 | tf_op jit(solution)/shard_map/ppermute | solution.py:417
  5.0 7.9 %collective-permute-start = (bf16[2,144,512]{2,1,0:T(8,128)(2,1)}, bf16[2,144,512]{2,1,0:T(8,128)(2,1)S(1)}, u32[]{:S(2)}, u32[]{:S(2)}) collective-permute-start(bf16[2,144,512]{2,1,0:T(8,128)(2,1)} %get-tuple-element.26.refs_0_), channel_id=1, source_target_pairs={{16,0},{18,2},{20,4},{22,6},{24,8},{26,10},{28,12},{30,14},{32,16}... | collective-permute-start | bytes 884744 | tf_op jit(solution)/shard_map/ppermute | solution.py:409
  8.9 8.9 %collective-permute-start.4 = (bf16[2,144,512]{2,1,0:T(8,128)(2,1)}, bf16[2,144,512]{2,1,0:T(8,128)(2,1)S(1)}, u32[]{:S(2)}, u32[]{:S(2)}) collective-permute-start(bf16[2,144,512]{2,1,0:T(8,128)(2,1)} %get-tuple-element.26.refs_0_), channel_id=1, source_target_pairs={{48,0},{50,2},{52,4},{54,6},{56,8},{58,10},{60,12},{62,14},{0,16},... | collective-permute-start | bytes 884744 | tf_op jit(solution)/shard_map/ppermute | solution.py:409
  8.9 12.1 %collective-permute-start.5 = (bf16[2,144,512]{2,1,0:T(8,128)(2,1)}, bf16[2,144,512]{2,1,0:T(8,128)(2,1)S(1)}, u32[]{:S(2)}, u32[]{:S(2)}) collective-permute-start(bf16[2,144,512]{2,1,0:T(8,128)(2,1)} %get-tuple-element.26.refs_0_), channel_id=1, source_target_pairs={{32,0},{34,2},{36,4},{38,6},{40,8},{42,10},{44,12},{46,14},{48,16}... | collective-permute-start | bytes 884744 | tf_op jit(solution)/shard_map/ppermute | solution.py:409
  12.9 8.6 %collective-permute-start.1 = (bf16[2,144,512]{2,1,0:T(8,128)(2,1)S(1)}, bf16[2,144,512]{2,1,0:T(8,128)(2,1)S(1)}, u32[]{:S(2)}, u32[]{:S(2)}) collective-permute-start(bf16[2,144,512]{2,1,0:T(8,128)(2,1)S(1)} %collective-permute-done.refs_1_), channel_id=1, source_target_pairs={{3,1},{5,3},{7,5},{9,7},{11,9},{13,11},{15,13},{1,15},{19,17},{21,... | collective-permute-start | bytes 884744 | tf_op jit(solution)/shard_map/ppermute | solution.py:409
  17.8 8.7 %collective-permute-start.6 = (bf16[2,144,512]{2,1,0:T(8,128)(2,1)S(1)}, bf16[2,144,512]{2,1,0:T(8,128)(2,1)S(1)}, u32[]{:S(2)}, u32[]{:S(2)}) collective-permute-start(bf16[2,144,512]{2,1,0:T(8,128)(2,1)S(1)} %collective-permute-done.4.refs_2_), channel_id=1, source_target_pairs={{15,1},{1,3},{3,5},{5,7},{7,9},{9,11},{11,13},{13,15},{31,17},{17,... | collective-permute-start | bytes 884744 | tf_op jit(solution)/shard_map/ppermute | solution.py:409
  19.7 10.9 %copy-start.5 = (s32[6]{0:T(128)S(1)}, s32[6]{0:T(128)}, u32[]{:S(2)}) copy-start(s32[6]{0:T(128)} %source.1) | copy-start | bytes 76
  21.0 16.6 %copy-start.1 = (bf16[6,2,128,512]{3,2,1,0:T(8,128)(2,1)S(1)}, bf16[6,2,128,512]{3,2,1,0:T(8,128)(2,1)}, u32[]{:S(2)}) copy-start(bf16[6,2,128,512]{3,2,1,0:T(8,128)(2,1)} %refs_15_.1) | copy-start | bytes 4718596
  21.0 16.6 %copy-start.2 = (bf16[6,2,64,128]{3,2,1,0:T(8,128)(2,1)S(1)}, bf16[6,2,64,128]{3,2,1,0:T(8,128)(2,1)}, u32[]{:S(2)}) copy-start(bf16[6,2,64,128]{3,2,1,0:T(8,128)(2,1)} %refs_16_.1) | copy-start | bytes 589828
  27.5 16.3 %collective-permute-start.8 = (bf16[4,2,144,512]{3,2,1,0:T(8,128)(2,1)S(1)}, bf16[4,2,144,512]{3,2,1,0:T(8,128)(2,1)S(1)}, u32[]{:S(2)}, u32[]{:S(2)}) collective-permute-start(bf16[4,2,144,512]{3,2,1,0:T(8,128)(2,1)S(1)} %stack1.1.refs_6_), channel_id=1, source_target_pairs={{2,0},{4,2},{6,4},{8,6},{10,8},{12,10},{14,12},{0,14},{18,16},{20,... | collective-permute-start | bytes 3538952 | tf_op jit(solution)/shard_map/ppermute | solution.py:409
  30.6 16.3 %collective-permute-start.9 = (bf16[4,2,144,512]{3,2,1,0:T(8,128)(2,1)S(1)}, bf16[4,2,144,512]{3,2,1,0:T(8,128)(2,1)S(1)}, u32[]{:S(2)}, u32[]{:S(2)}) collective-permute-start(bf16[4,2,144,512]{3,2,1,0:T(8,128)(2,1)S(1)} %stack1.1.refs_6_), channel_id=1, source_target_pairs={{14,0},{0,2},{2,4},{4,6},{6,8},{8,10},{10,12},{12,14},{30,16},{16,... | collective-permute-start | bytes 3538952 | tf_op jit(solution)/shard_map/ppermute | solution.py:409
  30.6 3.6 %collective-permute-start.10 = (s32[6]{0:T(128)S(1)}, s32[6]{0:T(128)S(1)}, u32[]{:S(2)}, u32[]{:S(2)}) collective-permute-start(s32[6]{0:T(128)S(1)} %copy-done.5), channel_id=1, source_target_pairs={{0,192},{64,0},{128,64},{192,128},{1,193},{65,1},{129,65},{193,129... | collective-permute-start | bytes 80 | tf_op jit(solution)/shard_map/ppermute | solution.py:413
  33.1 3.9 %collective-permute-start.11 = (s32[6]{0:T(128)S(1)}, s32[6]{0:T(128)S(1)}, u32[]{:S(2)}, u32[]{:S(2)}) collective-permute-start(s32[6]{0:T(128)S(1)} %copy-done.5), channel_id=1, source_target_pairs={{0,128},{64,192},{128,0},{192,64},{1,129},{65,193},{129,1},{193,65... | collective-permute-start | bytes 80 | tf_op jit(solution)/shard_map/ppermute | solution.py:413
  33.6 3.9 %collective-permute-start.12 = (s32[6]{0:T(128)S(1)}, s32[6]{0:T(128)S(1)}, u32[]{:S(2)}, u32[]{:S(2)}) collective-permute-start(s32[6]{0:T(128)S(1)} %copy-done.5), channel_id=1, source_target_pairs={{0,64},{64,128},{128,192},{192,0},{1,65},{65,129},{129,193},{193,1... | collective-permute-start | bytes 80 | tf_op jit(solution)/shard_map/ppermute | solution.py:413
  46.9 17.4 %copy-start.4 = (s32[114]{0:T(128)S(1)}, s32[114]{0:T(128)}, u32[]{:S(2)}) copy-start(s32[114]{0:T(128)} %get-tuple-element.27.refs_0_) | copy-start | bytes 1372
  47.0 18.4 %collective-permute-start.13 = (bf16[4,2,144,512]{3,2,1,0:T(8,128)(2,1)S(1)}, bf16[4,2,144,512]{3,2,1,0:T(8,128)(2,1)S(1)}, u32[]{:S(2)}, u32[]{:S(2)}) collective-permute-start(bf16[4,2,144,512]{3,2,1,0:T(8,128)(2,1)S(1)} %get-tuple-element.32), channel_id=1, source_target_pairs={{2,0},{4,2},{6,4},{8,6},{10,8},{12,10},{14,12},{0,14},{18,16},{20,... | collective-permute-start | bytes 3538952 | tf_op jit(solution)/shard_map/ppermute | solution.py:409
  47.1 18.3 %collective-permute-start.14 = (bf16[4,2,144,512]{3,2,1,0:T(8,128)(2,1)S(1)}, bf16[4,2,144,512]{3,2,1,0:T(8,128)(2,1)S(1)}, u32[]{:S(2)}, u32[]{:S(2)}) collective-permute-start(bf16[4,2,144,512]{3,2,1,0:T(8,128)(2,1)S(1)} %get-tuple-element.33), channel_id=1, source_target_pairs={{14,0},{0,2},{2,4},{4,6},{6,8},{8,10},{10,12},{12,14},{30,16},{16,... | collective-permute-start | bytes 3538952 | tf_op jit(solution)/shard_map/ppermute | solution.py:409
  48.6 16.9 %collective-permute-start.16 = (bf16[2,2,144,512]{3,2,1,0:T(8,128)(2,1)S(1)}, bf16[2,2,144,512]{3,2,1,0:T(8,128)(2,1)S(1)}, u32[]{:S(2)}, u32[]{:S(2)}) collective-permute-start(bf16[2,2,144,512]{3,2,1,0:T(8,128)(2,1)S(1)} %get-tuple-element.30.refs_3_), channel_id=1, source_target_pairs={{0,128},{64,192},{128,0},{192,64},{1,129},{65,193},{129,1},{193,65... | collective-permute-start | bytes 1769480 | tf_op jit(solution)/shard_map/ppermute | solution.py:413
  51.3 11.0 %collective-permute-start.2 = (bf16[2,144,512]{2,1,0:T(8,128)(2,1)S(1)}, bf16[2,144,512]{2,1,0:T(8,128)(2,1)S(1)}, u32[]{:S(2)}, u32[]{:S(2)}) collective-permute-start(bf16[2,144,512]{2,1,0:T(8,128)(2,1)S(1)} %collective-permute-done.1.refs_5_.refs_0_.refs_10_), channel_id=1, source_target_pairs={{3,1},{5,3},{7,5},{9,7},{11,9},{13,11},{15,13},{1,15},{19,17},{21,... | collective-permute-start | bytes 884744 | tf_op jit(solution)/shard_map/ppermute | solution.py:409
  53.2 11.1 %collective-permute-start.15 = (bf16[2,144,512]{2,1,0:T(8,128)(2,1)S(1)}, bf16[2,144,512]{2,1,0:T(8,128)(2,1)S(1)}, u32[]{:S(2)}, u32[]{:S(2)}) collective-permute-start(bf16[2,144,512]{2,1,0:T(8,128)(2,1)S(1)} %collective-permute-done.6.refs_6_.refs_1_.refs_11_), channel_id=1, source_target_pairs={{15,1},{1,3},{3,5},{5,7},{7,9},{9,11},{11,13},{13,15},{31,17},{17,... | collective-permute-start | bytes 884744 | tf_op jit(solution)/shard_map/ppermute | solution.py:409
  62.3 9.6 %copy-start = (bf16[6,2,128,512]{3,2,1,0:T(8,128)(2,1)S(1)}, bf16[6,2,128,512]{3,2,1,0:T(8,128)(2,1)}, u32[]{:S(2)}) copy-start(bf16[6,2,128,512]{3,2,1,0:T(8,128)(2,1)} %refs_2_.5) | copy-start | bytes 4718596
  62.3 3.1 %collective-permute-start.17 = (bf16[6,2,128,64]{3,2,1,0:T(8,128)(2,1)S(1)}, bf16[6,2,128,64]{3,2,1,0:T(8,128)(2,1)S(1)}, u32[]{:S(2)}, u32[]{:S(2)}) collective-permute-start(bf16[6,2,128,64]{3,2,1,0:T(8,128)(2,1)S(1)} %reshape.3.refs_4_.refs_3_), channel_id=1, source_target_pairs={{0,1},{1,0},{2,3},{3,2},{4,5},{5,4},{6,7},{7,6},{8,9},{9,8},{10,11... | collective-permute-start | bytes 589832 | tf_op jit(solution)/shard_map/ppermute | solution.py:417
  64.3 1.1 %collective-permute-start.3 = (s32[114]{0:T(128)S(1)}, s32[114]{0:T(128)S(1)}, u32[]{:S(2)}, u32[]{:S(2)}) collective-permute-start(s32[114]{0:T(128)S(1)} %copy-done.4), channel_id=1, source_target_pairs={{0,1},{1,0},{2,3},{3,2},{4,5},{5,4},{6,7},{7,6},{8,9},{9,8},{10,11... | collective-permute-start | bytes 1376 | tf_op jit(solution)/shard_map/ppermute | solution.py:417
  65.7 20.1 %collective-permute-start.18 = (bf16[4,2,144,512]{3,2,1,0:T(8,128)(2,1)S(1)}, bf16[4,2,144,512]{3,2,1,0:T(8,128)(2,1)S(1)}, u32[]{:S(2)}, u32[]{:S(2)}) collective-permute-start(bf16[4,2,144,512]{3,2,1,0:T(8,128)(2,1)S(1)} %get-tuple-element.35), channel_id=1, source_target_pairs={{2,0},{4,2},{6,4},{8,6},{10,8},{12,10},{14,12},{0,14},{18,16},{20,... | collective-permute-start | bytes 3538952 | tf_op jit(solution)/shard_map/ppermute | solution.py:409
  65.7 20.0 %collective-permute-start.19 = (bf16[4,2,144,512]{3,2,1,0:T(8,128)(2,1)S(1)}, bf16[4,2,144,512]{3,2,1,0:T(8,128)(2,1)S(1)}, u32[]{:S(2)}, u32[]{:S(2)}) collective-permute-start(bf16[4,2,144,512]{3,2,1,0:T(8,128)(2,1)S(1)} %get-tuple-element.36), channel_id=1, source_target_pairs={{14,0},{0,2},{2,4},{4,6},{6,8},{8,10},{10,12},{12,14},{30,16},{16,... | collective-permute-start | bytes 3538952 | tf_op jit(solution)/shard_map/ppermute | solution.py:409
  67.2 11.8 %collective-permute-start.20 = (bf16[2,144,512]{2,1,0:T(8,128)(2,1)S(1)}, bf16[2,144,512]{2,1,0:T(8,128)(2,1)S(1)}, u32[]{:S(2)}, u32[]{:S(2)}) collective-permute-start(bf16[2,144,512]{2,1,0:T(8,128)(2,1)S(1)} %collective-permute-done.2.refs_0_.refs_8_), channel_id=1, source_target_pairs={{3,1},{5,3},{7,5},{9,7},{11,9},{13,11},{15,13},{1,15},{19,17},{21,... | collective-permute-start | bytes 884744 | tf_op jit(solution)/shard_map/ppermute | solution.py:409
  69.1 16.6 %collective-permute-start.21 = (bf16[2,2,144,512]{3,2,1,0:T(8,128)(2,1)S(1)}, bf16[2,2,144,512]{3,2,1,0:T(8,128)(2,1)S(1)}, u32[]{:S(2)}, u32[]{:S(2)}) collective-permute-start(bf16[2,2,144,512]{3,2,1,0:T(8,128)(2,1)S(1)} %get-tuple-element.29.refs_2_), channel_id=1, source_target_pairs={{0,64},{64,128},{128,192},{192,0},{1,65},{65,129},{129,193},{193,1... | collective-permute-start | bytes 1769480 | tf_op jit(solution)/shard_map/ppermute | solution.py:413
  70.6 15.1 %collective-permute-start.22 = (bf16[2,2,144,512]{3,2,1,0:T(8,128)(2,1)S(1)}, bf16[2,2,144,512]{3,2,1,0:T(8,128)(2,1)S(1)}, u32[]{:S(2)}, u32[]{:S(2)}) collective-permute-start(bf16[2,2,144,512]{3,2,1,0:T(8,128)(2,1)S(1)} %get-tuple-element.31.refs_4_), channel_id=1, source_target_pairs={{0,192},{64,0},{128,64},{192,128},{1,193},{65,1},{129,65},{193,129... | collective-permute-start | bytes 1769480 | tf_op jit(solution)/shard_map/ppermute | solution.py:413
  85.8 11.8 %collective-permute-start.23 = (bf16[2,2,144,512]{3,2,1,0:T(8,128)(2,1)S(1)}, bf16[2,2,144,512]{3,2,1,0:T(8,128)(2,1)S(1)}, u32[]{:S(2)}, u32[]{:S(2)}) collective-permute-start(bf16[2,2,144,512]{3,2,1,0:T(8,128)(2,1)S(1)} %get-tuple-element.38), channel_id=1, source_target_pairs={{2,0},{4,2},{6,4},{8,6},{10,8},{12,10},{14,12},{0,14},{18,16},{20,... | collective-permute-start | bytes 1769480 | tf_op jit(solution)/shard_map/ppermute | solution.py:409
  85.9 13.2 %collective-permute-start.24 = (bf16[2,2,144,512]{3,2,1,0:T(8,128)(2,1)S(1)}, bf16[2,2,144,512]{3,2,1,0:T(8,128)(2,1)S(1)}, u32[]{:S(2)}, u32[]{:S(2)}) collective-permute-start(bf16[2,2,144,512]{3,2,1,0:T(8,128)(2,1)S(1)} %get-tuple-element.39), channel_id=1, source_target_pairs={{14,0},{0,2},{2,4},{4,6},{6,8},{8,10},{10,12},{12,14},{30,16},{16,... | collective-permute-start | bytes 1769480 | tf_op jit(solution)/shard_map/ppermute | solution.py:409
  87.4 10.2 %collective-permute-start.25 = (bf16[2,144,512]{2,1,0:T(8,128)(2,1)S(1)}, bf16[2,144,512]{2,1,0:T(8,128)(2,1)S(1)}, u32[]{:S(2)}, u32[]{:S(2)}) collective-permute-start(bf16[2,144,512]{2,1,0:T(8,128)(2,1)S(1)} %collective-permute-done.20.refs_0_.refs_10_), channel_id=1, source_target_pairs={{33,1},{35,3},{37,5},{39,7},{41,9},{43,11},{45,13},{47,15},{49,17}... | collective-permute-start | bytes 884744 | tf_op jit(solution)/shard_map/ppermute | solution.py:409
  103.6 4.3 %collective-permute-start.26 = (bf16[6,2,128,640]{3,2,1,0:T(8,128)(2,1)S(1)}, bf16[6,2,128,640]{3,2,1,0:T(8,128)(2,1)S(1)}, u32[]{:S(2)}, u32[]{:S(2)}) collective-permute-start(bf16[6,2,128,640]{3,2,1,0:T(8,128)(2,1)S(1)} %flash_far_par.1.refs_14_), channel_id=1, source_target_pairs={{0,1},{1,0},{2,3},{3,2},{4,5},{5,4},{6,7},{7,6},{8,9},{9,8},{10,11... | collective-permute-start | bytes 5898248 | tf_op jit(solution)/shard_map/ppermute | solution.py:417
  (1 other events, 1.0 us)
